TPU v7x, 256 devices: a whole 4x4x8 slice. The times are simulated.
256 devices in a mesh: ctx: 8 (over z), head: 32 (over x, y, core).
Axes of the slice: x: 4, y: 4, z: 8, core: 2. Of those that a mesh axis runs over, the one named last changes fastest.
Arguments:
- query_raw: bfloat16 [16384, 2048], P(('ctx', 'head')), may hold values from -6 to 6
- key_raw: bfloat16 [16384, 2048], P(('ctx', 'head')), may hold values from -6 to 6
- value_raw: bfloat16 [16384, 4096], P(('ctx', 'head')), may hold values from -6 to 6
- decay_raw: bfloat16 [16384, 32], P(('ctx', 'head'))
- beta_raw: bfloat16 [16384, 32], P(('ctx', 'head'))
- decay_base: float32 [32], replicated
- decay_bias: float32 [32], replicated, may hold values from -0.5 to 0.5
- doc_lengths: int32 [4], replicated, may hold values from 1 to 8192, 16384 in all
- out_grad: bfloat16 [16384, 4096], P(('ctx', 'head')), may hold values from -6 to 6
Outputs:
- output: bfloat16 [16384, 4096], P(('ctx', 'head'))
- query_grad: bfloat16 [16384, 2048], P(('ctx', 'head'))
- key_grad: bfloat16 [16384, 2048], P(('ctx', 'head'))
- value_grad: bfloat16 [16384, 4096], P(('ctx', 'head'))
- decay_grad: bfloat16 [16384, 32], P(('ctx', 'head'))
- beta_grad: bfloat16 [16384, 32], P(('ctx', 'head'))
All inputs are finite; a program needn't handle non-finite values.
Results may differ from a plain program's by a relative error of at most 0.02.
Values may be sent and summed in bfloat16 or wider, within the bound.
No kernel may reach another device: no remote copies, remote signals or barrier semaphores. Data moves between devices by JAX's collectives and lax.ppermute only.
A program may use at most 128 MiB of HBM per device.

v0:
```python
import functools

import jax
import jax.numpy as jnp
from jax import lax
from jax.experimental import pallas as pl
from jax.experimental.pallas import tpu as pltpu
from jax.sharding import PartitionSpec as P

VALUE_HEAD_COUNT = 32
NK = 16
DK = 128
DV = 128
GROUP = 128
GATE_ROWS = 16
STEP_BLOCKS = 4
VMEM_BYTES = 60 * 1024 * 1024

bf16 = jnp.bfloat16
f32 = jnp.float32


def contract(left, right, left_dim, right_dim):
    return lax.dot_general(
        left.astype(bf16),
        right.astype(bf16),
        (((left_dim,), (right_dim,)), ((), ())),
        preferred_element_type=f32,
    )


def mm(left, right):
    return contract(left, right, 1, 0)


def mm_nt(left, right):
    return contract(left, right, 1, 1)


def mm_tn(left, right):
    return contract(left, right, 0, 0)


def exact(left, right, left_dim, right_dim):
    return lax.dot_general(
        left,
        right,
        (((left_dim,), (right_dim,)), ((), ())),
        preferred_element_type=f32,
        precision=lax.Precision.HIGHEST,
    )


def iota(shape, dim):
    return lax.broadcasted_iota(jnp.int32, shape, dim)


def segment_of(positions, starts):
    count = jnp.zeros(positions.shape, jnp.int32)
    for start in starts:
        count = count + jnp.where(positions >= start, 1, 0)
    return count


def pick_column(table, block):
    lane = iota(table.shape, 1)
    return jnp.sum(jnp.where(lane == block, table, 0.0), axis=1, keepdims=True)


def block_gates(block, ints_ref, gate_ref, column_ref):
    starts = [ints_ref[1 + j] for j in range(4)]
    first = ints_ref[0] * 16 * GROUP + block * GROUP
    cum_row = gate_ref[0, pl.ds(block, 1), :]
    beta_row = gate_ref[1, pl.ds(block, 1), :]
    cum_col = pick_column(column_ref[0], block)
    beta_col = pick_column(column_ref[1], block)
    seg_row = segment_of(first + iota((1, GROUP), 1), starts)
    seg_col = segment_of(first + iota((GROUP, 1), 0), starts)
    before = segment_of(jnp.full((1, 1), first - 1, jnp.int32), starts)
    row, col = iota((GROUP, GROUP), 0), iota((GROUP, GROUP), 1)
    joined = (row >= col) & (seg_col == seg_row)
    spread = jnp.where(joined, cum_col - cum_row, 0.0)
    weighted = jnp.where(joined, jnp.exp(spread), 0.0) * beta_row
    entry = jnp.where(seg_col == before, jnp.exp(cum_col), 0.0)
    cum_last = cum_col[GROUP - 1 :, :]
    same_last = seg_col == seg_col[GROUP - 1 :, :]
    last = (
        jnp.where(same_last, jnp.exp(jnp.where(same_last, cum_last - cum_col, 0.0)), 0.0) * beta_col
    )
    return weighted, entry, last, row, col


def inverse_root(raw):
    return lax.rsqrt(jnp.sum(raw * raw, axis=1, keepdims=True) + 1e-06)


def block_rows(x_ref, local, part):
    return jnp.concatenate(
        [x_ref[2 * local + half, 64 * part : 64 * part + 64, :] for half in range(2)], axis=0
    )


def normed(x_ref, local):
    query_raw = block_rows(x_ref, local, 0).astype(f32)
    key_raw = block_rows(x_ref, local, 1).astype(f32)
    query_root, key_root = inverse_root(query_raw), inverse_root(key_raw)
    query = query_raw * query_root * DK ** (-0.5)
    keys = key_raw * key_root
    return query_raw, key_raw, query_root, key_root, query.astype(bf16), keys.astype(bf16)


def triangular_inverse(strict, row, col):
    differ = row ^ col
    eye = jnp.where(differ == 0, 1.0, 0.0)
    inverse = eye - jnp.where(differ == 1, strict, 0.0)
    for level in range(1, 7):
        size = 1 << level
        between = jnp.where((differ >= size) & (differ < 2 * size), strict, 0.0).astype(bf16)
        held = inverse.astype(bf16)
        inverse = inverse - mm(mm(held, between), held)
    held = inverse.astype(bf16)
    upper = strict.astype(bf16)
    lower = (strict - upper.astype(f32)).astype(bf16)
    rest = eye - held.astype(f32) - mm(upper, held) - mm(lower, held)
    return held.astype(f32) + mm(held, rest)


def tables_kernel(
    ints_ref,
    floats_ref,
    gates_in_ref,
    x_ref,
    send_ref,
    gate_ref,
    column_ref,
    fresh_ref,
    out_ref,
    push_ref,
    maps_ref,
    prefix_ref,
    prefix_free_ref,
    suffix_ref,
    suffix_free_ref,
    step_ref,
    term_ref,
    carry_ref,
):
    here = pl.program_id(0)

    @pl.when(here == 0)
    def prologue():
        tail = gates_in_ref[...].astype(f32)
        paired = tail.reshape(16, 2, GATE_ROWS, 128)
        lane = iota((16, GATE_ROWS, 128), 2)
        rows = iota((16, GATE_ROWS, 128), 1)
        tail = jnp.where(lane < 64, paired[:, 0], paired[:, 1])
        decay_raw = jnp.sum(jnp.where(rows == 0, tail, 0.0), axis=1) + floats_ref[1]
        beta_raw = jnp.sum(jnp.where(rows == 1, tail, 0.0), axis=1)
        rate = -jnp.exp(jnp.full((16, 128), floats_ref[0], f32))
        decay_log = rate * (
            jnp.maximum(decay_raw, 0.0) + jnp.log1p(jnp.exp(-jnp.abs(decay_raw)))
        )
        row, col = iota((128, 128), 0), iota((128, 128), 1)
        upto = jnp.where(row <= col, 1.0, 0.0)
        eye = jnp.where(row == col, 1.0, 0.0)
        cumulative = exact(decay_log, upto, 1, 0)
        beta = jax.nn.sigmoid(beta_raw)
        gate_ref[0] = cumulative
        gate_ref[1] = beta
        gate_ref[2] = rate * jax.nn.sigmoid(decay_raw)
        padding = jnp.zeros((112, 128), f32)
        column_ref[0] = exact(eye, jnp.concatenate([cumulative, padding], 0), 1, 1)
        column_ref[1] = exact(eye, jnp.concatenate([beta, padding], 0), 1, 1)
        carry_ref[...] = jnp.concatenate([jnp.zeros((DK, DV), f32), eye], 1)

    for local in range(STEP_BLOCKS):
        block = here * STEP_BLOCKS + local
        weighted, entry, last, row, col = block_gates(block, ints_ref, gate_ref, column_ref)
        _, _, _, _, query, keys = normed(x_ref, local)
        values = block_rows(x_ref, local, 2)
        grads = block_rows(x_ref, local, 3)
        both = mm_nt(jnp.concatenate([keys, query], 0), keys)
        strict = jnp.where(row > col, weighted * both[:GROUP], 0.0)
        inverse = triangular_inverse(strict, row, col).astype(bf16)
        mixing = (weighted * both[GROUP:]).astype(bf16)
        keys_entry = (keys.astype(f32) * entry).astype(bf16)
        keys_last = (keys.astype(f32) * last).astype(bf16)
        first = mm(inverse, jnp.concatenate([values, keys_entry], 1))
        fresh, seen = first[:, :DV], first[:, DV:].astype(bf16)
        pair = jnp.concatenate([fresh.astype(bf16), seen], 1)
        mixed = mm(mixing, pair)
        read = (entry * query.astype(f32) - mixed[:, DV:]).astype(bf16)
        written = mm_tn(keys_last, pair)
        back = mm_tn(mixing, grads)
        pushed = mm_tn(inverse, jnp.concatenate([back.astype(bf16), keys_last], 1))
        step = written[:, DV:].astype(bf16)
        fresh_ref[local] = fresh
        out_ref[local] = mixed[:, :DV]
        push_ref[local] = pushed[:, :DV]
        maps_ref[local, 0] = seen
        maps_ref[local, 1] = read
        maps_ref[local, 2] = pushed[:, DV:].astype(bf16)
        step_ref[block] = step
        term_ref[block] = mm_tn(read, grads)
        carried = carry_ref[...]
        prefix_free_ref[local] = carried[:, :DV]
        prefix_ref[local] = carried[:, DV:].astype(bf16)
        last_entry = entry[GROUP - 1 :, :]
        moved = last_entry * carried - mm(step, carried)
        carry_ref[...] = moved + jnp.concatenate(
            [written[:, :DV], jnp.zeros((DK, DK), f32)], 1
        )
        term_ref[16 + block] = jnp.broadcast_to(last_entry, (DK, DV))

    @pl.when(here == pl.num_programs(0) - 1)
    def epilogue():
        row, col = iota((128, 128), 0), iota((128, 128), 1)
        eye = jnp.where(row == col, 1.0, 0.0)
        adjoint = jnp.concatenate([jnp.zeros((DK, DV), f32), eye], 1)
        for block in range(15, -1, -1):
            suffix_free_ref[block] = adjoint[:, :DV]
            suffix_ref[block] = adjoint[:, DV:].astype(bf16)
            scale = jnp.concatenate([term_ref[16 + block]] * 2, 1)
            moved = scale * adjoint - mm_tn(step_ref[block], adjoint)
            adjoint = moved + jnp.concatenate([term_ref[block], jnp.zeros((DK, DK), f32)], 1)
        free = carry_ref[:, :DV].astype(bf16)
        total = carry_ref[:, DV:].astype(bf16)
        term = adjoint[:, :DV].astype(bf16)
        for other in range(8):
            send_ref[other, :DK] = total
            send_ref[other, DK:] = jnp.where(ints_ref[0] < other, free, term)


def tables(ints, floats, received):
    blocks = received.shape[0] // 2
    steps = blocks // STEP_BLOCKS
    wide = jax.ShapeDtypeStruct((blocks, GROUP, DV), f32)
    half = jax.ShapeDtypeStruct((blocks, DK, DV), bf16)
    by_step = pl.BlockSpec((STEP_BLOCKS, GROUP, DV), lambda i: (i, 0, 0))
    whole = lambda *shape: pl.BlockSpec(shape, lambda i: (0,) * len(shape))
    return pl.pallas_call(
        tables_kernel,
        grid=(steps,),
        in_specs=[
            pl.BlockSpec(memory_space=pltpu.SMEM),
            pl.BlockSpec(memory_space=pltpu.SMEM),
            pl.BlockSpec((2 * blocks, GATE_ROWS, 128), lambda i: (0, 256 // GATE_ROWS, 0)),
            pl.BlockSpec((2 * STEP_BLOCKS, 256 + GATE_ROWS, 128), lambda i: (i, 0, 0)),
        ],
        out_specs=[
            whole(8, 256, 128),
            whole(3, blocks, 128),
            whole(2, 128, 128),
            by_step,
            by_step,
            by_step,
            pl.BlockSpec((STEP_BLOCKS, 3, GROUP, DV), lambda i: (i, 0, 0, 0)),
            by_step,
            by_step,
            whole(blocks, DK, DV),
            whole(blocks, DK, DV),
        ],
        out_shape=[
            jax.ShapeDtypeStruct((8, 256, 128), bf16),
            jax.ShapeDtypeStruct((3, blocks, 128), f32),
            jax.ShapeDtypeStruct((2, 128, 128), f32),
            wide,
            wide,
            wide,
            jax.ShapeDtypeStruct((blocks, 3, GROUP, DV), bf16),
            half,
            wide,
            half,
            wide,
        ],
        scratch_shapes=[
            pltpu.VMEM((blocks, DK, DK), bf16),
            pltpu.VMEM((2 * blocks, DK, DV), f32),
            pltpu.VMEM((DK, DV + DK), f32),
        ],
        compiler_params=pltpu.CompilerParams(
            dimension_semantics=("arbitrary",), vmem_limit_bytes=VMEM_BYTES
        ),
        name="tables",
    )(ints, floats, received, received)


def split_two(state):
    high = state.astype(bf16)
    return jnp.concatenate([high, (state - high.astype(f32)).astype(bf16)], 1)


def gradients_kernel(
    ints_ref,
    x_ref,
    shards_ref,
    gate_ref,
    column_ref,
    fresh_ref,
    out_ref,
    push_ref,
    maps_ref,
    prefix_ref,
    prefix_free_ref,
    suffix_ref,
    suffix_free_ref,
    y_ref,
    ends_ref,
):
    here = pl.program_id(0)

    @pl.when(here == 0)
    def prologue():
        me = ints_ref[0]
        state = jnp.zeros((DK, DV), f32)
        adjoint = jnp.zeros((DK, DV), f32)
        for k in range(7):
            moved = mm(shards_ref[k, :DK], split_two(state))
            new = moved[:, :DV] + moved[:, DV:] + shards_ref[k, DK:].astype(f32)
            state = jnp.where(k < me, new, state)
            at = 7 - k
            moved = mm_tn(shards_ref[at, :DK], split_two(adjoint))
            new = moved[:, :DV] + moved[:, DV:] + shards_ref[at, DK:].astype(f32)
            adjoint = jnp.where(at > me, new, adjoint)
        ends_ref[0] = state.astype(bf16)
        ends_ref[1] = adjoint.astype(bf16)

    lane = iota((GROUP, 8), 1)
    sublane = iota((8, GROUP), 0)
    change_cols = jnp.zeros((GROUP, 8), f32)
    beta_cols = jnp.zeros((GROUP, 8), f32)
    column_sums = jnp.zeros((8, GROUP), f32)
    for local in range(STEP_BLOCKS):
        block = here * STEP_BLOCKS + local
        weighted, entry, last, row, col = block_gates(block, ints_ref, gate_ref, column_ref)
        query_raw, key_raw, query_root, key_root, query, keys = normed(x_ref, local)
        grads = block_rows(x_ref, local, 3)
        state = prefix_free_ref[local] + mm(prefix_ref[local], ends_ref[0])
        adjoint = suffix_free_ref[local] + mm(suffix_ref[local], ends_ref[1])
        state_low, adjoint_low = state.astype(bf16), adjoint.astype(bf16)
        read = mm(maps_ref[local, 0:2].reshape(2 * GROUP, DK), state_low)
        fresh = (fresh_ref[local] - read[:GROUP]).astype(bf16)
        outputs = out_ref[local] + read[GROUP:]
        pushed = push_ref[local] + mm(maps_ref[local, 2], adjoint_low)
        sides = jnp.concatenate([grads, pushed.astype(bf16)], 0)
        on_fresh = mm_nt(sides, fresh)
        on_state = mm_nt(sides, state_low)
        on_adjoint = mm_nt(fresh, adjoint_low)
        both = mm_nt(jnp.concatenate([keys, query], 0), keys)
        mix_term = weighted * on_fresh[:GROUP]
        key_term = jnp.where(row > col, -weighted * on_fresh[GROUP:], 0.0)
        query_entry = entry * on_state[:GROUP]
        key_entry = -entry * on_state[GROUP:]
        key_last = last * on_adjoint
        stacked = jnp.concatenate([mix_term.astype(bf16), key_term.astype(bf16)], 0)
        direct = mm(stacked, keys)
        turned = mm_tn(stacked, jnp.concatenate([query, keys], 0))
        query_grad = query_entry + direct[:GROUP]
        key_grad = key_entry + key_last + direct[GROUP:] + turned
        query_wide, key_wide = query.astype(f32), keys.astype(f32)
        table = mix_term * both[GROUP:] + key_term * both[:GROUP]
        last_sums = jnp.sum(key_wide * key_last, axis=1, keepdims=True)
        change = (
            jnp.sum(table + query_wide * query_entry + key_wide * key_entry, axis=1, keepdims=True)
            - last_sums
        )
        extra = jnp.sum(last_sums, axis=0, keepdims=True) + entry[GROUP - 1 :, :] * jnp.sum(
            jnp.sum(adjoint * state, axis=1, keepdims=True), axis=0, keepdims=True
        )
        change = change + jnp.where(iota((GROUP, 1), 0) == GROUP - 1, extra, 0.0)
        change_cols = jnp.where(lane == local, change, change_cols)
        beta_cols = jnp.where(lane == local, last_sums, beta_cols)
        column_sums = jnp.where(
            sublane == local, jnp.sum(table, axis=0, keepdims=True), column_sums
        )
        query_grad = query_grad * DK ** (-0.5)
        query_dot = jnp.sum(query_grad * query_raw, axis=1, keepdims=True)
        key_dot = jnp.sum(key_grad * key_raw, axis=1, keepdims=True)
        query_back = query_root * query_grad - query_raw * (
            query_root * query_root * query_root * query_dot
        )
        key_back = key_root * key_grad - key_raw * (key_root * key_root * key_root * key_dot)
        for half in range(2):
            rows = slice(64 * half, 64 * half + 64)
            at = 2 * local + half
            y_ref[at, 0:64, :] = outputs[rows].astype(bf16)
            y_ref[at, 64:128, :] = query_back[rows].astype(bf16)
            y_ref[at, 128:192, :] = key_back[rows].astype(bf16)
            y_ref[at, 192:256, :] = pushed[rows].astype(bf16)

    row, col = iota((GROUP, GROUP), 0), iota((GROUP, GROUP), 1)
    after = jnp.where(row >= col, 1.0, 0.0)
    eye = jnp.where(row == col, 1.0, 0.0)
    decay_rows = exact(change_cols, after, 0, 0) - exact(column_sums, after, 1, 0)
    beta_rows = exact(beta_cols, eye, 0, 0) + column_sums
    for local in range(STEP_BLOCKS):
        block = here * STEP_BLOCKS + local
        decay_grad = decay_rows[local : local + 1] * gate_ref[2, pl.ds(block, 1), :]
        beta_grad = beta_rows[local : local + 1] * (1.0 - gate_ref[1, pl.ds(block, 1), :])
        rows = iota((GATE_ROWS, 128), 0)
        tail = jnp.where(rows == 0, decay_grad, jnp.where(rows == 1, beta_grad, 0.0)).astype(bf16)
        for half in range(2):
            y_ref[2 * local + half, 256:, :] = tail


def gradients(ints, received, shards, *made):
    blocks = received.shape[0] // 2
    steps = blocks // STEP_BLOCKS
    by_step = pl.BlockSpec((STEP_BLOCKS, GROUP, DV), lambda i: (i, 0, 0))
    whole = lambda *shape: pl.BlockSpec(shape, lambda i: (0,) * len(shape))
    rows_spec = pl.BlockSpec((2 * STEP_BLOCKS, 256 + GATE_ROWS, 128), lambda i: (i, 0, 0))
    return pl.pallas_call(
        gradients_kernel,
        grid=(steps,),
        in_specs=[
            pl.BlockSpec(memory_space=pltpu.SMEM),
            rows_spec,
            whole(8, 256, 128),
            whole(3, blocks, 128),
            whole(2, 128, 128),
            by_step,
            by_step,
            by_step,
            pl.BlockSpec((STEP_BLOCKS, 3, GROUP, DV), lambda i: (i, 0, 0, 0)),
            by_step,
            by_step,
            by_step,
            by_step,
        ],
        out_specs=rows_spec,
        out_shape=jax.ShapeDtypeStruct(received.shape, bf16),
        scratch_shapes=[pltpu.VMEM((2, DK, DV), bf16)],
        compiler_params=pltpu.CompilerParams(
            dimension_semantics=("arbitrary",), vmem_limit_bytes=VMEM_BYTES
        ),
        name="gradients",
    )(ints, received, shards, *made)


def pack_kernel(query_ref, key_ref, value_ref, decay_ref, beta_ref, grad_ref, x_ref):
    row, col = iota((64, 128), 0), iota((64, 128), 1)
    twice = jnp.where((col == row) | (col == row + 64), 1.0, 0.0).astype(bf16)
    decay = mm_tn(decay_ref[...], twice)
    beta = mm_tn(beta_ref[...], twice)
    rows = iota((GATE_ROWS, 128), 0)
    for head in range(VALUE_HEAD_COUNT):
        shared = slice(DK * (head // 2), DK * (head // 2) + DK)
        own = slice(DV * head, DV * head + DV)
        x_ref[head, 0:64, :] = query_ref[:, shared]
        x_ref[head, 64:128, :] = key_ref[:, shared]
        x_ref[head, 128:192, :] = value_ref[:, own]
        x_ref[head, 192:256, :] = grad_ref[:, own]
        x_ref[head, 256:, :] = jnp.where(
            rows == 0,
            decay[head : head + 1],
            jnp.where(rows == 1, beta[head : head + 1], 0.0),
        ).astype(bf16)


def pack(query, key, value, decay, beta, grad):
    return pl.pallas_call(
        pack_kernel,
        out_shape=jax.ShapeDtypeStruct((VALUE_HEAD_COUNT, 256 + GATE_ROWS, 128), bf16),
        compiler_params=pltpu.CompilerParams(vmem_limit_bytes=VMEM_BYTES),
        name="pack",
    )(query, key, value, decay, beta, grad)


def unpack_kernel(ints_ref, y_ref, out_ref, query_ref, key_ref, value_ref, decay_ref, beta_ref):
    row, col = iota((128, 64), 0), iota((128, 64), 1)
    select = jnp.where(row == col + 64 * ints_ref[5], 1.0, 0.0).astype(bf16)
    for head in range(VALUE_HEAD_COUNT):
        own = slice(DV * head, DV * head + DV)
        out_ref[:, own] = y_ref[head, 0:64, :]
        value_ref[:, own] = y_ref[head, 192:256, :]
    for head in range(NK):
        shared = slice(DK * head, DK * head + DK)
        for part, ref in ((1, query_ref), (2, key_ref)):
            rows = slice(64 * part, 64 * part + 64)
            summed = y_ref[2 * head, rows, :].astype(f32) + y_ref[2 * head + 1, rows, :].astype(f32)
            ref[:, shared] = summed.astype(bf16)
    tail = y_ref[:, 256:, :].astype(f32)
    rows = iota(tail.shape, 1)
    for index, ref in ((0, decay_ref), (1, beta_ref)):
        picked = jnp.sum(jnp.where(rows == index, tail, 0.0), axis=1)
        ref[...] = contract(select, picked, 0, 1).astype(bf16)


def unpack(ints, returned):
    wide = jax.ShapeDtypeStruct((64, VALUE_HEAD_COUNT * DV), bf16)
    narrow = jax.ShapeDtypeStruct((64, NK * DK), bf16)
    gates = jax.ShapeDtypeStruct((64, VALUE_HEAD_COUNT), bf16)
    vmem = pl.BlockSpec(memory_space=pltpu.VMEM)
    return pl.pallas_call(
        unpack_kernel,
        in_specs=[pl.BlockSpec(memory_space=pltpu.SMEM), vmem],
        out_specs=[vmem] * 6,
        out_shape=[wide, narrow, narrow, wide, gates, gates],
        compiler_params=pltpu.CompilerParams(vmem_limit_bytes=VMEM_BYTES),
        name="unpack",
    )(ints, returned)


def local(
    query_raw,
    key_raw,
    value_raw,
    decay_raw,
    beta_raw,
    decay_base,
    decay_bias,
    doc_lengths,
    out_grad,
):
    head = lax.axis_index("head")
    shard = lax.axis_index("ctx")
    sent = pack(query_raw, key_raw, value_raw, decay_raw, beta_raw, out_grad)
    received = lax.all_to_all(sent, "head", split_axis=0, concat_axis=0, tiled=True)
    ends = [jnp.sum(doc_lengths[:j]) for j in range(4)]
    ints = jnp.stack([shard.astype(jnp.int32), *ends, (head % 2).astype(jnp.int32)])
    floats = jnp.stack(
        [
            lax.dynamic_index_in_dim(decay_base, head, keepdims=False),
            lax.dynamic_index_in_dim(decay_bias, head, keepdims=False),
        ]
    )
    send, *made = tables(ints, floats, received)
    shards = lax.all_to_all(send, "ctx", split_axis=0, concat_axis=0, tiled=True)
    back = gradients(ints, received, shards, *made)
    returned = lax.all_to_all(back, "head", split_axis=0, concat_axis=0, tiled=True)
    output, query_grad, key_grad, value_grad, decay_grad, beta_grad = unpack(ints, returned)
    return (output, query_grad, key_grad, value_grad, decay_grad, beta_grad)


def solution(mesh):
    placed = (
        P(("ctx", "head"), None),
        P(("ctx", "head"), None),
        P(("ctx", "head"), None),
        P(("ctx", "head"), None),
        P(("ctx", "head"), None),
        P(),
        P(),
        P(),
        P(("ctx", "head"), None),
    )
    return jax.shard_map(
        local,
        mesh=mesh,
        in_specs=placed,
        out_specs=(P(("ctx", "head"), None),) * 6,
        check_vma=False,
    )
```

profile of v0, /device:TPU:1, one launch (start us, length us, event | category | flops | bytes accessed | tf_op | source)
XLA Modules:
  0.0 169.8 jit_solution(17349155650344191186)
XLA Ops:
  0.6 1.4 copy.15.decay_ref
  2.0 1.4 copy.16.beta_ref
  3.4 3.2 %pack.1 = bf16[32,272,128]{2,1,0:T(8,128)(2,1)} custom-call(bf16[64,2048]{1,0:T(8,128)(2,1)} %query_ref.1, bf16[64,2048]{1,0:T(8,128)(2,1)} %key_ref.1, bf16[64,4096]{1,0:T(8,128)(2,1)} %value_ref.1, bf16[64,32]{1,0:T(8,128)(2,1)} %copy.15.decay_ref, bf16[64,32]{1,0:T(8,128)(2,1)} %copy.16.beta_ref, bf16[64,4096]{1,0:T(8,128)(2,1)} %grad_ref.1), custom_call_target="tpu_custom_call" | custom-call | tf_op jit(solution)/shard_map/pack/pallas_call | solution.py:461
  6.6 0.0 copy-start.2
  6.6 0.0 copy-start.3
  6.6 0.0 copy-start.1
  6.6 8.7 %all-to-all-start = ((bf16[32,272,128]{2,1,0:T(8,128)(2,1)}), bf16[32,272,128]{2,1,0:T(8,128)(2,1)S(1)}, u32[]{:S(2)}, u32[]{:S(2)}) async-start(bf16[32,272,128]{2,1,0:T(8,128)(2,1)} %pack.1), calls=%async_computation | async-start | bytes 4456448 | tf_op jit(solution)/shard_map/all_to_all | solution.py:518
  15.3 0.0 copy-done.2
  15.3 0.6 dynamic_slice.8
  15.9 0.0 copy-done.3
  15.9 0.6 dynamic_slice.7
  16.5 0.0 copy-done.1
  16.5 0.6 slice_reduce_fusion
  17.1 0.6 slice_reduce_fusion.1
  17.8 1.9 %stack.25.ints_ref = s32[6]{0:T(128)} concatenate(s32[1]{0:T(128)} %bitcast, s32[1]{0:T(128)} %constant.26.clone.1, s32[1]{0:T(128)S(1)} %bitcast.5, s32[1]{0:T(128)} %bitcast.1, s32[1]{0:T(128)} %bitcast.2, s32[1]{0:T(128)} %bitcast.3), dimensions={0} | concatenate | bytes 48 | tf_op jit(solution)/shard_map/stack | solution.py:520
  19.7 1.9 %pad_maximum_fusion.floats_ref = f32[2]{0:T(128)} fusion(f32[1]{0:T(128)} %dynamic_slice.8, f32[1]{0:T(128)} %dynamic_slice.7), kind=kLoop, calls=%fused_computation | loop fusion | flops 2 | bytes 16 | tf_op jit(solution)/shard_map/stack | solution.py:521
  21.6 23.4 %all-to-all-done.gates_in_ref.x_ref = bf16[32,272,128]{2,1,0:T(8,128)(2,1)S(1)} async-done(((bf16[32,272,128]{2,1,0:T(8,128)(2,1)}), bf16[32,272,128]{2,1,0:T(8,128)(2,1)S(1)}, u32[]{:S(2)}, u32[]{:S(2)}) %all-to-all-start) | async-done | bytes 2228256 | tf_op jit(solution)/shard_map/all_to_all | solution.py:518
  45.0 0.0 copy-start
  45.0 1.4 copy-done
  46.4 42.6 %tables.1 = (bf16[8,256,128]{2,1,0:T(8,128)(2,1)}, f32[3,16,128]{2,1,0:T(8,128)}, f32[2,128,128]{2,1,0:T(8,128)}, f32[16,128,128]{2,1,0:T(8,128)}, f32[16,128,12...) custom-call(s32[6]{0:T(128)} %stack.25.ints_ref, ...), custom_call_target="tpu_custom_call" | custom-call | tf_op jit(solution)/shard_map/tables/pallas_call | solution.py:241
  89.0 24.0 %all_to_all.15.shards_ref = bf16[8,256,128]{2,1,0:T(8,128)(2,1)} all-to-all(bf16[8,256,128]{2,1,0:T(8,128)(2,1)} %get-tuple-element.17), channel_id=1, replica_groups=mesh['ctx'=8,'head'=32] {'ctx'}, dimensions={0} | all-to-all | bytes 1048576 | tf_op jit(solution)/shard_map/all_to_all | solution.py:528
  113.0 13.6 %gradients.1 = bf16[32,272,128]{2,1,0:T(8,128)(2,1)} custom-call(s32[6]{0:T(128)} %stack.25.ints_ref, bf16[32,272,128]{2,1,0:T(8,128)(2,1)} %copy-done, bf16[8,256,128]{2,1,0:T(8,128)(2,1)} %all_to_all.15.shards_ref, f32[3,16,128]{2,1,0:T(8,128)} %get-tuple-element.18.gate_ref, f32[2,128,128]{2,1,0:T(8,128)} %get-tuple-element.19.column_ref, ...), custom_call_target="tpu_custom_call" | custom-call | tf_op jit(solution)/shard_map/gradients/pallas_call | solution.py:412
  126.6 37.4 %all_to_all.16.y_ref = bf16[32,272,128]{2,1,0:T(8,128)(2,1)} all-to-all(bf16[32,272,128]{2,1,0:T(8,128)(2,1)} %gradients.1), channel_id=1, replica_groups=mesh['ctx'=8,'head'=32] {'head'}, dimensions={0} | all-to-all | bytes 4456448 | tf_op jit(solution)/shard_map/all_to_all | solution.py:530
  164.0 3.0 %unpack.1 = (bf16[64,4096]{1,0:T(8,128)(2,1)}, bf16[64,2048]{1,0:T(8,128)(2,1)}, bf16[64,2048]{1,0:T(8,128)(2,1)}, bf16[64,4096]{1,0:T(8,128)(2,1)}, bf16[64,32]{1,0:T(8,128)(2,1)}, /*index=5*/bf16[64,32]{1,0:T(8,128)(2,1)}) custom-call(s32[6]{0:T(128)} %stack.25.ints_ref, bf16[32,272,128]{2,1,0:T(8,128)(2,1)} %all_to_all.16.y_ref), custom_call_target="tpu_custom_call" | custom-call | tf_op jit(solution)/shard_map/unpack/pallas_call | solution.py:494
  167.0 1.4 copy.17
  168.4 1.4 copy.18
Async XLA Ops:
  6.6 8.8 %copy-start.2 = (f32[32]{0:T(128)S(1)}, f32[32]{0:T(128)}, u32[]{:S(2)}) copy-start(f32[32]{0:T(128)} %param.15) | copy-start | bytes 388
  6.6 9.4 %copy-start.3 = (f32[32]{0:T(128)S(1)}, f32[32]{0:T(128)}, u32[]{:S(2)}) copy-start(f32[32]{0:T(128)} %param.14) | copy-start | bytes 388
  6.6 9.9 %copy-start.1 = (s32[4]{0:T(128)S(1)}, s32[4]{0:T(128)}, u32[]{:S(2)}) copy-start(s32[4]{0:T(128)} %param.16) | copy-start | bytes 52
  6.6 38.4 %all-to-all-start = ((bf16[32,272,128]{2,1,0:T(8,128)(2,1)}), bf16[32,272,128]{2,1,0:T(8,128)(2,1)S(1)}, u32[]{:S(2)}, u32[]{:S(2)}) async-start(bf16[32,272,128]{2,1,0:T(8,128)(2,1)} %pack.1), calls=%async_computation | async-start | bytes 4456448 | tf_op jit(solution)/shard_map/all_to_all | solution.py:518
  45.0 1.4 copy-start
where the time goes:
time: 170 us
  Pallas kernels  62.3 us (37%)
  blocking collectives  61.5 us (36%)
  waiting for transfers between devices  23.4 us (14%)
  local copies, waits for them, and re-layouts  10 us (6%)
  starting transfers between devices  8.73 us (5%)
  other arithmetic  3.14 us (2%)
    pallas_call x1, Pallas kernels, tables(): pl.pallas_call(tables_kernel, grid=(steps,), in_specs=[pl.BlockSpec(memor...  42.6 us
    all_to_all x1, blocking collectives, local(): lax.all_to_all(back, 'head', split_axis=0, concat_axis=0, tiled=True)  37.4 us
    all_to_all x1, blocking collectives, local(): lax.all_to_all(send, 'ctx', split_axis=0, concat_axis=0, tiled=True)  24 us
    all_to_all x1, waiting for transfers between devices, local(): lax.all_to_all(sent, 'head', split_axis=0, concat_axis=0, tiled=True)  23.4 us
    pallas_call x1, Pallas kernels, gradients(): pl.pallas_call(gradients_kernel, grid=(steps,), in_specs=[pl.BlockSpec(me...  13.6 us
    all_to_all x1, starting transfers between devices, local(): lax.all_to_all(sent, 'head', split_axis=0, concat_axis=0, tiled=True)  8.73 us
    unnamed x10, local copies, waits for them, and re-layouts  4.15 us
  transfers between devices with their start and end apart: 1, of which 1 were waited for; matrix products, arithmetic and copies ran while one was open for 4% of the time, Pallas kernels for 0%

commit v1 on v0

v1 whole, which is shorter than its diff:
```python
import functools

import jax
import jax.numpy as jnp
from jax import lax
from jax.experimental import pallas as pl
from jax.experimental.pallas import tpu as pltpu
from jax.sharding import PartitionSpec as P

VALUE_HEAD_COUNT = 32
NK = 16
DK = 128
DV = 128
GROUP = 128
GATE_ROWS = 16
PACK_HEADS = 16
STATE_BLOCKS = 8
OUTPUT_BLOCKS = 8
GRADIENT_BLOCKS = 4
BLOCKS = 16
SHARDS = 8
VMEM_BYTES = 60 * 1024 * 1024

bf16 = jnp.bfloat16
f32 = jnp.float32


def contract(left, right, left_dim, right_dim):
    return lax.dot_general(
        left.astype(bf16),
        right.astype(bf16),
        (((left_dim,), (right_dim,)), ((), ())),
        preferred_element_type=f32,
    )


def mm(left, right):
    return contract(left, right, 1, 0)


def mm_nt(left, right):
    return contract(left, right, 1, 1)


def mm_tn(left, right):
    return contract(left, right, 0, 0)


def exact(left, right, left_dim, right_dim):
    return lax.dot_general(
        left,
        right,
        (((left_dim,), (right_dim,)), ((), ())),
        preferred_element_type=f32,
        precision=lax.Precision.HIGHEST,
    )


def iota(shape, dim):
    return lax.broadcasted_iota(jnp.int32, shape, dim)


def segment_of(positions, starts):
    count = jnp.zeros(positions.shape, jnp.int32)
    for start in starts:
        count = count + jnp.where(positions >= start, 1, 0)
    return count


def pick_column(table, block):
    lane = iota(table.shape, 1)
    return jnp.sum(jnp.where(lane == block, table, 0.0), axis=1, keepdims=True)


def block_gates(block, ints_ref, gate_ref, column_ref):
    starts = [ints_ref[1 + j] for j in range(4)]
    first = ints_ref[0] * 16 * GROUP + block * GROUP
    cum_row = gate_ref[0, pl.ds(block, 1), :]
    beta_row = gate_ref[1, pl.ds(block, 1), :]
    cum_col = pick_column(column_ref[0], block)
    beta_col = pick_column(column_ref[1], block)
    seg_row = segment_of(first + iota((1, GROUP), 1), starts)
    seg_col = segment_of(first + iota((GROUP, 1), 0), starts)
    before = segment_of(jnp.full((1, 1), first - 1, jnp.int32), starts)
    row, col = iota((GROUP, GROUP), 0), iota((GROUP, GROUP), 1)
    joined = (row >= col) & (seg_col == seg_row)
    spread = jnp.where(joined, cum_col - cum_row, 0.0)
    weighted = jnp.where(joined, jnp.exp(spread), 0.0) * beta_row
    entry = jnp.where(seg_col == before, jnp.exp(cum_col), 0.0)
    cum_last = cum_col[GROUP - 1 :, :]
    same_last = seg_col == seg_col[GROUP - 1 :, :]
    last = (
        jnp.where(same_last, jnp.exp(jnp.where(same_last, cum_last - cum_col, 0.0)), 0.0) * beta_col
    )
    return weighted, entry, last


def inverse_root(raw):
    return lax.rsqrt(jnp.sum(raw * raw, axis=1, keepdims=True) + 1e-06)


def block_rows(ref, block, part):
    return jnp.concatenate(
        [ref[2 * block + half, 64 * part : 64 * part + 64, :] for half in range(2)], axis=0
    )


def eye_of(size):
    return jnp.where(iota((size, size), 0) == iota((size, size), 1), 1.0, 0.0)


def split_rows(matrix):
    high = matrix.astype(bf16)
    return jnp.concatenate([high, (matrix - high.astype(f32)).astype(bf16)], 0)


def cost(units):
    return pl.CostEstimate(
        flops=units * BLOCKS * 2 * 128**3 * 8, bytes_accessed=1 << 20, transcendentals=0
    )


def triangular_inverses(stricts, row, col):
    differ = row ^ col
    eye = jnp.where(differ == 0, 1.0, 0.0)
    inverses = [eye - jnp.where(differ == 1, strict, 0.0) for strict in stricts]
    for level in range(1, 7):
        size = 1 << level
        band = (differ >= size) & (differ < 2 * size)
        held = [inverse.astype(bf16) for inverse in inverses]
        half = [
            mm(one, jnp.where(band, strict, 0.0)) for one, strict in zip(held, stricts)
        ]
        step = [mm(one, other) for one, other in zip(half, held)]
        inverses = [inverse - one for inverse, one in zip(inverses, step)]
    held = [inverse.astype(bf16) for inverse in inverses]
    upper = [strict.astype(bf16) for strict in stricts]
    lower = [(strict - one.astype(f32)).astype(bf16) for strict, one in zip(stricts, upper)]
    rest = [mm(one, other) for one, other in zip(upper, held)]
    fine = [mm(one, other) for one, other in zip(lower, held)]
    rest = [
        eye - one.astype(f32) - high - low for one, high, low in zip(held, rest, fine)
    ]
    return [one.astype(f32) + mm(one, other) for one, other in zip(held, rest)]


def maps_kernel(
    ints_ref,
    floats_ref,
    x_ref,
    gate_ref,
    column_ref,
    keys_ref,
    inverse_ref,
    seen_ref,
    back_ref,
    step_ref,
    prefix_ref,
    suffix_ref,
    total_ref,
):
    tail = x_ref[:, 64:, :].astype(f32)
    paired = tail.reshape(BLOCKS, 2, GATE_ROWS, 128)
    lane = iota((BLOCKS, GATE_ROWS, 128), 2)
    rows = iota((BLOCKS, GATE_ROWS, 128), 1)
    tail = jnp.where(lane < 64, paired[:, 0], paired[:, 1])
    decay_raw = jnp.sum(jnp.where(rows == 0, tail, 0.0), axis=1) + floats_ref[1]
    beta_raw = jnp.sum(jnp.where(rows == 1, tail, 0.0), axis=1)
    rate = -jnp.exp(jnp.full((BLOCKS, 128), floats_ref[0], f32))
    decay_log = rate * (jnp.maximum(decay_raw, 0.0) + jnp.log1p(jnp.exp(-jnp.abs(decay_raw))))
    row, col = iota((128, 128), 0), iota((128, 128), 1)
    eye = eye_of(128)
    cumulative = exact(decay_log, jnp.where(row <= col, 1.0, 0.0), 1, 0)
    beta = jax.nn.sigmoid(beta_raw)
    gate_ref[0] = cumulative
    gate_ref[1] = beta
    gate_ref[2] = rate * jax.nn.sigmoid(decay_raw)
    padding = jnp.zeros((128 - BLOCKS, 128), f32)
    column_ref[0] = exact(eye, jnp.concatenate([cumulative, padding], 0), 1, 1)
    column_ref[1] = exact(eye, jnp.concatenate([beta, padding], 0), 1, 1)

    each = range(BLOCKS)
    gates = [block_gates(i, ints_ref, gate_ref, column_ref) for i in each]
    raws = [block_rows(x_ref, i, 0).astype(f32) for i in each]
    keys = [(raw * inverse_root(raw)).astype(bf16) for raw in raws]
    both = [mm_nt(one, one) for one in keys]
    stricts = [jnp.where(row > col, gates[i][0] * both[i], 0.0) for i in each]
    inverses = [one.astype(bf16) for one in triangular_inverses(stricts, row, col)]
    keys_entry = [(keys[i].astype(f32) * gates[i][1]).astype(bf16) for i in each]
    keys_last = [(keys[i].astype(f32) * gates[i][2]).astype(bf16) for i in each]
    seen = [mm(inverses[i], keys_entry[i]).astype(bf16) for i in each]
    back = [mm_tn(inverses[i], keys_last[i]).astype(bf16) for i in each]
    steps = [mm_tn(keys_last[i], seen[i]).astype(bf16) for i in each]
    scales = [gates[i][1][GROUP - 1 :, :] for i in each]
    for i in each:
        keys_ref[i] = keys[i]
        inverse_ref[i] = inverses[i]
        seen_ref[i] = seen[i]
        back_ref[i] = back[i]
        step_ref[i] = steps[i]
        gate_ref[3, i : i + 1, :] = jnp.broadcast_to(scales[i], (1, 128))
    forward, backward = eye, eye
    for i in each:
        other = BLOCKS - 1 - i
        forward_low, backward_low = forward.astype(bf16), backward.astype(bf16)
        prefix_ref[i] = forward_low
        suffix_ref[other] = backward_low
        forward = scales[i] * forward - mm(steps[i], forward_low)
        backward = scales[other] * backward - mm_tn(steps[other], backward_low)
    total_ref[...] = forward.astype(bf16)


def maps(ints, floats, keys_got):
    half = jax.ShapeDtypeStruct((BLOCKS, GROUP, DK), bf16)
    vmem = pl.BlockSpec(memory_space=pltpu.VMEM)
    smem = pl.BlockSpec(memory_space=pltpu.SMEM)
    return pl.pallas_call(
        maps_kernel,
        in_specs=[smem, smem, vmem],
        out_specs=[vmem] * 10,
        out_shape=[
            jax.ShapeDtypeStruct((4, BLOCKS, 128), f32),
            jax.ShapeDtypeStruct((2, 128, 128), f32),
            *[half] * 7,
            jax.ShapeDtypeStruct((DK, DK), bf16),
        ],
        compiler_params=pltpu.CompilerParams(vmem_limit_bytes=VMEM_BYTES),
        cost_estimate=cost(20),
        name="maps",
    )(ints, floats, keys_got)


def compose_kernel(ints_ref, *refs):
    total_refs, (forward_ref, backward_ref) = refs[: SHARDS - 1], refs[SHARDS - 1 :]
    me = ints_ref[0]
    forward, backward = eye_of(DK), eye_of(DK)
    for k in range(1, SHARDS):
        at = slice(DK * (k - 1), DK * k)
        forward_ref[:, at] = jnp.where(k <= me, forward, 0.0).astype(bf16)
        backward_ref[:, at] = jnp.where(me + k < SHARDS, backward, 0.0).astype(bf16)
        if k < SHARDS - 1:
            moved = mm(split_rows(forward), total_refs[k - 1][...])
            forward = moved[:DK] + moved[DK:]
            moved = mm_nt(split_rows(backward), total_refs[SHARDS - 1 - k][...])
            backward = moved[:DK] + moved[DK:]


def compose(ints, totals):
    vmem = pl.BlockSpec(memory_space=pltpu.VMEM)
    smem = pl.BlockSpec(memory_space=pltpu.SMEM)
    wide = jax.ShapeDtypeStruct((DK, (SHARDS - 1) * DK), bf16)
    return pl.pallas_call(
        compose_kernel,
        in_specs=[smem] + [vmem] * (SHARDS - 1),
        out_specs=[vmem] * 2,
        out_shape=[wide, wide],
        compiler_params=pltpu.CompilerParams(vmem_limit_bytes=VMEM_BYTES),
        cost_estimate=cost(2),
        name="compose",
    )(ints, *totals)


def states_kernel(
    ints_ref,
    x_ref,
    gate_ref,
    column_ref,
    keys_ref,
    inverse_ref,
    seen_ref,
    step_ref,
    fresh_ref,
    out_ref,
    push_ref,
    read_ref,
    prefix_ref,
    suffix_ref,
    *rest,
):
    send_refs, (term_ref, carry_ref) = rest[: SHARDS - 1], rest[SHARDS - 1 :]
    here = pl.program_id(0)

    @pl.when(here == 0)
    def prologue():
        carry_ref[...] = jnp.zeros((DK, DV), f32)

    each = range(STATE_BLOCKS)
    first = here * STATE_BLOCKS
    gates = [block_gates(first + i, ints_ref, gate_ref, column_ref) for i in each]
    raws = [block_rows(x_ref, i, 0).astype(f32) for i in each]
    queries = [(raw * inverse_root(raw) * DK ** (-0.5)).astype(bf16) for raw in raws]
    keys = [keys_ref[i] for i in each]
    grads = [block_rows(x_ref, i, 2) for i in each]
    mixing = [(gates[i][0] * mm_nt(queries[i], keys[i])).astype(bf16) for i in each]
    fresh = [mm(inverse_ref[i], block_rows(x_ref, i, 1)) for i in each]
    back = [mm_tn(mixing[i], grads[i]).astype(bf16) for i in each]
    pairs = [jnp.concatenate([fresh[i].astype(bf16), seen_ref[i]], 1) for i in each]
    mixed = [mm(mixing[i], pairs[i]) for i in each]
    keys_last = [(keys[i].astype(f32) * gates[i][2]).astype(bf16) for i in each]
    written = [mm_tn(keys_last[i], pairs[i][:, :DV]) for i in each]
    reads = [(gates[i][1] * queries[i].astype(f32) - mixed[i][:, DV:]).astype(bf16) for i in each]
    terms = [mm_tn(reads[i], grads[i]) for i in each]
    pushed = [mm_tn(inverse_ref[i], back[i]) for i in each]
    carried = carry_ref[...]
    for i in each:
        block = first + i
        fresh_ref[i] = pairs[i][:, :DV]
        out_ref[i] = mixed[i][:, :DV].astype(bf16)
        push_ref[i] = pushed[i].astype(bf16)
        read_ref[i] = reads[i]
        term_ref[block] = terms[i]
        carried_low = carried.astype(bf16)
        prefix_ref[i] = carried_low
        carried = (
            gate_ref[3, pl.ds(block, 1), :] * carried
            - mm(step_ref[block], carried_low)
            + written[i]
        )
    carry_ref[...] = carried

    @pl.when(here == pl.num_programs(0) - 1)
    def epilogue():
        adjoint = jnp.zeros((DK, DV), f32)
        for block in range(BLOCKS - 1, -1, -1):
            adjoint_low = adjoint.astype(bf16)
            suffix_ref[block] = adjoint_low
            adjoint = (
                gate_ref[3, block : block + 1, :] * adjoint
                - mm_tn(step_ref[block], adjoint_low)
                + term_ref[block]
            )
        for k, ref in enumerate(send_refs):
            ref[...] = jnp.where(
                ints_ref[0] + k + 1 < SHARDS, carry_ref[...], adjoint
            ).astype(bf16)


def whole(*shape):
    return pl.BlockSpec(shape, lambda i: (0,) * len(shape))


def stepped(count, *shape):
    return pl.BlockSpec((count, *shape), lambda i: (i,) + (0,) * len(shape))


def states(ints, others, gate, column, keys, inverse, seen, step):
    half = jax.ShapeDtypeStruct((BLOCKS, GROUP, DK), bf16)
    by_step = stepped(STATE_BLOCKS, GROUP, DK)
    square = jax.ShapeDtypeStruct((DK, DV), bf16)
    return pl.pallas_call(
        states_kernel,
        grid=(BLOCKS // STATE_BLOCKS,),
        in_specs=[
            pl.BlockSpec(memory_space=pltpu.SMEM),
            stepped(2 * STATE_BLOCKS, 192, 128),
            whole(4, BLOCKS, 128),
            whole(2, 128, 128),
            by_step,
            by_step,
            by_step,
            whole(BLOCKS, DK, DK),
        ],
        out_specs=[by_step] * 5 + [whole(BLOCKS, DK, DV)] + [whole(DK, DV)] * (SHARDS - 1),
        out_shape=[half] * 6 + [square] * (SHARDS - 1),
        scratch_shapes=[pltpu.VMEM((BLOCKS, DK, DV), f32), pltpu.VMEM((DK, DV), f32)],
        compiler_params=pltpu.CompilerParams(
            dimension_semantics=("arbitrary",), vmem_limit_bytes=VMEM_BYTES
        ),
        cost_estimate=cost(14),
        name="states",
    )(ints, others, gate, column, keys, inverse, seen, step)


def outputs_kernel(
    forward_ref,
    backward_ref,
    seen_ref,
    back_ref,
    prefix_map_ref,
    suffix_map_ref,
    fresh_ref,
    out_ref,
    push_ref,
    read_ref,
    prefix_ref,
    suffix_ref,
    *rest,
):
    end_refs, (y_ref, state_ref, adjoint_ref, made_ref, ends_ref) = (
        rest[: SHARDS - 1],
        rest[SHARDS - 1 :],
    )

    @pl.when(pl.program_id(0) == 0)
    def prologue():
        got = [ref[...] for ref in end_refs]
        ends_ref[0] = mm(forward_ref[...], jnp.concatenate(got, 0)).astype(bf16)
        ends_ref[1] = mm(backward_ref[...], jnp.concatenate(got[::-1], 0)).astype(bf16)

    each = range(OUTPUT_BLOCKS)
    state_end, adjoint_end = ends_ref[0], ends_ref[1]
    low = [
        (prefix_ref[i].astype(f32) + mm(prefix_map_ref[i], state_end)).astype(bf16) for i in each
    ]
    adjoints = [
        (suffix_ref[i].astype(f32) + mm(suffix_map_ref[i], adjoint_end)).astype(bf16) for i in each
    ]
    fresh = [fresh_ref[i].astype(f32) - mm(seen_ref[i], low[i]) for i in each]
    outputs = [out_ref[i].astype(f32) + mm(read_ref[i], low[i]) for i in each]
    pushed = [push_ref[i].astype(f32) + mm(back_ref[i], adjoints[i]) for i in each]
    for i in each:
        state_ref[i] = low[i]
        adjoint_ref[i] = adjoints[i]
        made_ref[i] = fresh[i].astype(bf16)
        for half in range(2):
            rows = slice(64 * half, 64 * half + 64)
            y_ref[2 * i + half, :64, :] = outputs[i][rows].astype(bf16)
            y_ref[2 * i + half, 64:, :] = pushed[i][rows].astype(bf16)


def outputs(forward, backward, blocks, ends):
    half = jax.ShapeDtypeStruct((BLOCKS, GROUP, DK), bf16)
    by_step = stepped(OUTPUT_BLOCKS, GROUP, DK)
    return pl.pallas_call(
        outputs_kernel,
        grid=(BLOCKS // OUTPUT_BLOCKS,),
        in_specs=[whole(DK, (SHARDS - 1) * DK)] * 2
        + [by_step] * 10
        + [whole(DK, DV)] * (SHARDS - 1),
        out_specs=[stepped(2 * OUTPUT_BLOCKS, 128, 128)] + [by_step] * 3,
        out_shape=[jax.ShapeDtypeStruct((2 * BLOCKS, 128, 128), bf16)] + [half] * 3,
        scratch_shapes=[pltpu.VMEM((2, DK, DV), bf16)],
        compiler_params=pltpu.CompilerParams(
            dimension_semantics=("arbitrary",), vmem_limit_bytes=VMEM_BYTES
        ),
        cost_estimate=cost(5),
        name="outputs",
    )(forward, backward, *blocks, *ends)


def gradients_kernel(
    ints_ref,
    keys_got_ref,
    others_ref,
    gate_ref,
    column_ref,
    keys_ref,
    y_ref,
    state_ref,
    adjoint_ref,
    made_ref,
    z_ref,
):
    here = pl.program_id(0)
    lane = iota((GROUP, 8), 1)
    sublane = iota((8, GROUP), 0)
    change_cols = jnp.zeros((GROUP, 8), f32)
    beta_cols = jnp.zeros((GROUP, 8), f32)
    column_sums = jnp.zeros((8, GROUP), f32)
    each = range(GRADIENT_BLOCKS)
    row, col = iota((GROUP, GROUP), 0), iota((GROUP, GROUP), 1)
    sides = [
        jnp.concatenate([block_rows(others_ref, i, 2), block_rows(y_ref, i, 1)], 0) for i in each
    ]
    on_fresh = [mm_nt(sides[i], made_ref[i]) for i in each]
    on_state = [mm_nt(sides[i], state_ref[i]) for i in each]
    on_adjoint = [mm_nt(made_ref[i], adjoint_ref[i]) for i in each]
    query_raws = [block_rows(others_ref, i, 0).astype(f32) for i in each]
    query_roots = [inverse_root(raw) for raw in query_raws]
    queries = [
        (query_raws[i] * query_roots[i] * DK ** (-0.5)).astype(bf16) for i in each
    ]
    keys = [keys_ref[i] for i in each]
    both = [mm_nt(jnp.concatenate([keys[i], queries[i]], 0), keys[i]) for i in each]
    gates = [
        block_gates(here * GRADIENT_BLOCKS + i, ints_ref, gate_ref, column_ref) for i in each
    ]
    mix_terms = [gates[i][0] * on_fresh[i][:GROUP] for i in each]
    key_terms = [jnp.where(row > col, -gates[i][0] * on_fresh[i][GROUP:], 0.0) for i in each]
    stacked = [
        jnp.concatenate([mix_terms[i].astype(bf16), key_terms[i].astype(bf16)], 0) for i in each
    ]
    direct = [mm(stacked[i], keys[i]) for i in each]
    turned = [mm_tn(stacked[i], jnp.concatenate([queries[i], keys[i]], 0)) for i in each]
    for i in each:
        _, entry, last = gates[i]
        query_raw, query_root = query_raws[i], query_roots[i]
        key_raw = block_rows(keys_got_ref, i, 0).astype(f32)
        key_root = inverse_root(key_raw)
        query_entry = entry * on_state[i][:GROUP]
        key_entry = -entry * on_state[i][GROUP:]
        key_last = last * on_adjoint[i]
        query_grad = query_entry + direct[i][:GROUP]
        key_grad = key_entry + key_last + direct[i][GROUP:] + turned[i]
        query_wide, key_wide = queries[i].astype(f32), keys[i].astype(f32)
        table = mix_terms[i] * both[i][GROUP:] + key_terms[i] * both[i][:GROUP]
        last_sums = jnp.sum(key_wide * key_last, axis=1, keepdims=True)
        change = (
            jnp.sum(table + query_wide * query_entry + key_wide * key_entry, axis=1, keepdims=True)
            - last_sums
        )
        overlap = adjoint_ref[i].astype(f32) * state_ref[i].astype(f32)
        extra = jnp.sum(last_sums, axis=0, keepdims=True) + entry[GROUP - 1 :, :] * jnp.sum(
            jnp.sum(overlap, axis=0, keepdims=True), axis=1, keepdims=True
        )
        change = change + jnp.where(iota((GROUP, 1), 0) == GROUP - 1, extra, 0.0)
        change_cols = jnp.where(lane == i, change, change_cols)
        beta_cols = jnp.where(lane == i, last_sums, beta_cols)
        column_sums = jnp.where(sublane == i, jnp.sum(table, axis=0, keepdims=True), column_sums)
        query_grad = query_grad * DK ** (-0.5)
        query_dot = jnp.sum(query_grad * query_raw, axis=1, keepdims=True)
        key_dot = jnp.sum(key_grad * key_raw, axis=1, keepdims=True)
        query_back = query_root * query_grad - query_raw * (
            query_root * query_root * query_root * query_dot
        )
        key_back = key_root * key_grad - key_raw * (key_root * key_root * key_root * key_dot)
        for half in range(2):
            rows = slice(64 * half, 64 * half + 64)
            z_ref[2 * i + half, 0:64, :] = query_back[rows].astype(bf16)
            z_ref[2 * i + half, 64:128, :] = key_back[rows].astype(bf16)

    after = jnp.where(row >= col, 1.0, 0.0)
    decay_rows = exact(change_cols, after, 0, 0) - exact(column_sums, after, 1, 0)
    beta_rows = exact(beta_cols, eye_of(GROUP), 0, 0) + column_sums
    for i in each:
        block = here * GRADIENT_BLOCKS + i
        decay_grad = decay_rows[i : i + 1] * gate_ref[2, pl.ds(block, 1), :]
        beta_grad = beta_rows[i : i + 1] * (1.0 - gate_ref[1, pl.ds(block, 1), :])
        rows = iota((GATE_ROWS, 128), 0)
        tail = jnp.where(rows == 0, decay_grad, jnp.where(rows == 1, beta_grad, 0.0)).astype(bf16)
        for half in range(2):
            z_ref[2 * i + half, 128:, :] = tail


def gradients(ints, keys_got, others, gate, column, keys, y, state, adjoint, made):
    by_step = stepped(GRADIENT_BLOCKS, GROUP, DK)
    rows = lambda count: stepped(2 * GRADIENT_BLOCKS, count, 128)
    return pl.pallas_call(
        gradients_kernel,
        grid=(BLOCKS // GRADIENT_BLOCKS,),
        in_specs=[
            pl.BlockSpec(memory_space=pltpu.SMEM),
            rows(64 + GATE_ROWS),
            rows(192),
            whole(4, BLOCKS, 128),
            whole(2, 128, 128),
            by_step,
            rows(128),
            by_step,
            by_step,
            by_step,
        ],
        out_specs=rows(128 + GATE_ROWS),
        out_shape=jax.ShapeDtypeStruct((2 * BLOCKS, 128 + GATE_ROWS, 128), bf16),
        compiler_params=pltpu.CompilerParams(
            dimension_semantics=("arbitrary",), vmem_limit_bytes=VMEM_BYTES
        ),
        cost_estimate=cost(14),
        name="gradients",
    )(ints, keys_got, others, gate, column, keys, y, state, adjoint, made)


def spec_wide():
    return pl.BlockSpec((64, PACK_HEADS * DV), lambda i: (0, i))


def spec_narrow():
    return pl.BlockSpec((64, PACK_HEADS * DK // 2), lambda i: (0, i))


def spec_gates():
    return pl.BlockSpec((PACK_HEADS, 64), lambda i: (i, 0))


def pack_keys_kernel(key_ref, decay_ref, beta_ref, x_ref):
    decay = jnp.concatenate([decay_ref[...].astype(f32)] * 2, 1)
    beta = jnp.concatenate([beta_ref[...].astype(f32)] * 2, 1)
    rows = iota((GATE_ROWS, 128), 0)
    for head in range(VALUE_HEAD_COUNT):
        x_ref[head, :64, :] = key_ref[:, DK * (head // 2) : DK * (head // 2) + DK]
        x_ref[head, 64:, :] = jnp.where(
            rows == 0,
            decay[head : head + 1],
            jnp.where(rows == 1, beta[head : head + 1], 0.0),
        ).astype(bf16)


def pack_keys(key, decay, beta):
    return pl.pallas_call(
        pack_keys_kernel,
        out_shape=jax.ShapeDtypeStruct((VALUE_HEAD_COUNT, 64 + GATE_ROWS, 128), bf16),
        compiler_params=pltpu.CompilerParams(vmem_limit_bytes=VMEM_BYTES),
        name="pack_keys",
    )(key, decay, beta)


def pack_others_kernel(query_ref, value_ref, grad_ref, x_ref):
    for head in range(PACK_HEADS):
        own = slice(DV * head, DV * head + DV)
        x_ref[head, 0:64, :] = query_ref[:, DK * (head // 2) : DK * (head // 2) + DK]
        x_ref[head, 64:128, :] = value_ref[:, own]
        x_ref[head, 128:192, :] = grad_ref[:, own]


def pack_others(query, value, grad):
    return pl.pallas_call(
        pack_others_kernel,
        grid=(VALUE_HEAD_COUNT // PACK_HEADS,),
        in_specs=[spec_narrow(), spec_wide(), spec_wide()],
        out_specs=stepped(PACK_HEADS, 192, 128),
        out_shape=jax.ShapeDtypeStruct((VALUE_HEAD_COUNT, 192, 128), bf16),
        compiler_params=pltpu.CompilerParams(vmem_limit_bytes=VMEM_BYTES),
        cost_estimate=cost(3),
        name="pack_others",
    )(query, value, grad)


def unpack_outputs_kernel(y_ref, out_ref, value_ref):
    for head in range(PACK_HEADS):
        own = slice(DV * head, DV * head + DV)
        out_ref[:, own] = y_ref[head, 0:64, :]
        value_ref[:, own] = y_ref[head, 64:128, :]


def unpack_outputs(returned):
    made = jax.ShapeDtypeStruct((64, VALUE_HEAD_COUNT * DV), bf16)
    return pl.pallas_call(
        unpack_outputs_kernel,
        grid=(VALUE_HEAD_COUNT // PACK_HEADS,),
        in_specs=[stepped(PACK_HEADS, 128, 128)],
        out_specs=[spec_wide()] * 2,
        out_shape=[made] * 2,
        compiler_params=pltpu.CompilerParams(vmem_limit_bytes=VMEM_BYTES),
        cost_estimate=cost(3),
        name="unpack_outputs",
    )(returned)


def unpack_gradients_kernel(ints_ref, z_ref, query_ref, key_ref, decay_ref, beta_ref):
    for head in range(PACK_HEADS // 2):
        shared = slice(DK * head, DK * head + DK)
        for part, ref in ((0, query_ref), (1, key_ref)):
            rows = slice(64 * part, 64 * part + 64)
            summed = z_ref[2 * head, rows, :].astype(f32) + z_ref[2 * head + 1, rows, :].astype(f32)
            ref[:, shared] = summed.astype(bf16)
    tail = z_ref[:, 128:, :].astype(f32)
    rows = iota(tail.shape, 1)
    for index, ref in ((0, decay_ref), (1, beta_ref)):
        picked = jnp.sum(jnp.where(rows == index, tail, 0.0), axis=1)
        ref[...] = jnp.where(ints_ref[5] == 0, picked[:, :64], picked[:, 64:]).astype(bf16)


def unpack_gradients(ints, returned):
    narrow = jax.ShapeDtypeStruct((64, NK * DK), bf16)
    gates = jax.ShapeDtypeStruct((VALUE_HEAD_COUNT, 64), bf16)
    return pl.pallas_call(
        unpack_gradients_kernel,
        grid=(VALUE_HEAD_COUNT // PACK_HEADS,),
        in_specs=[
            pl.BlockSpec(memory_space=pltpu.SMEM),
            stepped(PACK_HEADS, 128 + GATE_ROWS, 128),
        ],
        out_specs=[spec_narrow()] * 2 + [spec_gates()] * 2,
        out_shape=[narrow, narrow, gates, gates],
        compiler_params=pltpu.CompilerParams(vmem_limit_bytes=VMEM_BYTES),
        name="unpack_gradients",
    )(ints, returned)


def ring(parts, axis):
    return [
        lax.ppermute(part, axis, [(i, (i + k + 1) % SHARDS) for i in range(SHARDS)])
        for k, part in enumerate(parts)
    ]


def local(
    query_raw,
    key_raw,
    value_raw,
    decay_raw,
    beta_raw,
    decay_base,
    decay_bias,
    doc_lengths,
    out_grad,
):
    head = lax.axis_index("head")
    shard = lax.axis_index("ctx")
    ends = [jnp.sum(doc_lengths[:j]) for j in range(4)]
    ints = jnp.stack([shard.astype(jnp.int32), *ends, (head % 2).astype(jnp.int32)])
    floats = jnp.stack(
        [
            lax.dynamic_index_in_dim(decay_base, head, keepdims=False),
            lax.dynamic_index_in_dim(decay_bias, head, keepdims=False),
        ]
    )

    def to_heads(sent):
        return lax.all_to_all(sent, "head", split_axis=0, concat_axis=0, tiled=True)

    keys_got = to_heads(pack_keys(key_raw, decay_raw.T, beta_raw.T))
    others = to_heads(pack_others(query_raw, value_raw, out_grad))
    gate, column, keys, inverse, seen, back, step, prefix_map, suffix_map, total = maps(
        ints, floats, keys_got
    )
    forward, backward = compose(ints, ring([total] * (SHARDS - 1), "ctx"))
    others, forward, backward = lax.optimization_barrier((others, forward, backward))
    fresh, out, push, read, prefix, suffix, *sends = states(
        ints, others, gate, column, keys, inverse, seen, step
    )
    got = ring(sends, "ctx")
    y, state, adjoint, made = outputs(
        forward,
        backward,
        (seen, back, prefix_map, suffix_map, fresh, out, push, read, prefix, suffix),
        got,
    )
    z = gradients(ints, keys_got, others, gate, column, keys, y, state, adjoint, made)
    output, value_grad = unpack_outputs(to_heads(y))
    query_grad, key_grad, decay_grad, beta_grad = unpack_gradients(ints, to_heads(z))
    return (output, query_grad, key_grad, value_grad, decay_grad.T, beta_grad.T)


def solution(mesh):
    placed = (
        P(("ctx", "head"), None),
        P(("ctx", "head"), None),
        P(("ctx", "head"), None),
        P(("ctx", "head"), None),
        P(("ctx", "head"), None),
        P(),
        P(),
        P(),
        P(("ctx", "head"), None),
    )
    return jax.shard_map(
        local,
        mesh=mesh,
        in_specs=placed,
        out_specs=(P(("ctx", "head"), None),) * 6,
        check_vma=False,
    )
```

time: 170 us -> 153 us (0.900)
  blocking collectives: 61.5 us -> 0 us
  starting transfers between devices: 8.73 us -> 55.3 us
  Pallas kernels: 62.3 us -> 42 us
  waiting for transfers between devices: 23.4 us -> 43.1 us
  local copies, waits for them, and re-layouts: 10 us -> 7.88 us
    all_to_all x2 -> x0, blocking collectives: 61.5 us -> none  [the longest x1 37.4 us: local(): lax.all_to_all(back, 'head', split_axis=0, concat_axis=0, tiled=True)]
    ppermute x0 -> x14, starting transfers between devices: none -> 28.8 us  [ring(): lax.ppermute(part, axis, [(i, (i + k + 1) % SHARDS) for i in range(SHARDS)])]
    pallas_call x4 -> x9, Pallas kernels: 62.3 us -> 42 us  [the longest x1 9.82 us: states(): pl.pallas_call(states_kernel, grid=(BLOCKS // STATE_BLOCKS,), in_specs=[p...]
    all_to_all x1 -> x4, starting transfers between devices: 8.73 us -> 26.5 us  [to_heads(): return lax.all_to_all(sent, 'head', split_axis=0, concat_axis=0, tiled=True)]
    all_to_all x1 -> x4, waiting for transfers between devices: 23.4 us -> 35.9 us  [to_heads(): return lax.all_to_all(sent, 'head', split_axis=0, concat_axis=0, tiled=True)]
    ppermute x0 -> x14, waiting for transfers between devices: none -> 7.25 us  [ring(): lax.ppermute(part, axis, [(i, (i + k + 1) % SHARDS) for i in range(SHARDS)])]
    pallas_call x2 -> x0, local copies, waits for them, and re-layouts: 2.78 us -> none  [unpack(): pl.pallas_call(unpack_kernel, in_specs=[pl.BlockSpec(memory_space=pltpu.S...]
    unnamed x10 -> x42, local copies, waits for them, and re-layouts: 4.15 us -> 4.82 us
  transfers between devices with their start and end apart: 1 -> 18, of which waited for: 1 -> 7; matrix products, arithmetic and copies ran while one was open for 4% -> 4% of each run, Pallas kernels for 0% -> 16%
where the time goes in v1:
time: 153 us; the launch traced here: 152 us
  starting transfers between devices  55.3 us (36%)
  waiting for transfers between devices  43.1 us (28%)
  Pallas kernels  42 us (27%)
  local copies, waits for them, and re-layouts  7.88 us (5%)
  other arithmetic  3.14 us (2%)
    all_to_all x4, waiting for transfers between devices, to_heads(): return lax.all_to_all(sent, 'head', split_axis=0, concat_axis=0, tiled=True)  35.9 us
    ppermute x14, starting transfers between devices, ring(): lax.ppermute(part, axis, [(i, (i + k + 1) % SHARDS) for i in range(SHARDS)])  28.8 us
    all_to_all x4, starting transfers between devices, to_heads(): return lax.all_to_all(sent, 'head', split_axis=0, concat_axis=0, tiled=True)  26.5 us
    pallas_call x1, Pallas kernels, states(): pl.pallas_call(states_kernel, grid=(BLOCKS // STATE_BLOCKS,), in_specs=[p...  9.82 us
    pallas_call x1, Pallas kernels, maps(): pl.pallas_call(maps_kernel, in_specs=[smem, smem, vmem], out_specs=[vmem]...  8.83 us
    pallas_call x1, Pallas kernels, gradients(): pl.pallas_call(gradients_kernel, grid=(BLOCKS // GRADIENT_BLOCKS,), in_sp...  7.76 us
    ppermute x14, waiting for transfers between devices, ring(): lax.ppermute(part, axis, [(i, (i + k + 1) % SHARDS) for i in range(SHARDS)])  7.25 us
    unnamed x42, local copies, waits for them, and re-layouts  4.82 us
  transfers between devices with their start and end apart: 18, of which 7 were waited for; matrix products, arithmetic and copies ran while one was open for 4% of the time, Pallas kernels for 16%

profile of v1, /device:TPU:1, one launch (start us, length us, event | category | flops | bytes accessed | tf_op | source)
XLA Modules:
  0.0 152.3 jit_solution(3828236846871684871)
XLA Ops:
  0.6 1.9 %pack_keys.1 = bf16[32,80,128]{2,1,0:T(8,128)(2,1)} custom-call(bf16[64,2048]{1,0:T(8,128)(2,1)} %key_ref.1, bf16[32,64]{1,0:T(8,128)(2,1)} %bitcast.9, bf16[32,64]{1,0:T(8,128)(2,1)} %bitcast.10), custom_call_target="tpu_custom_call" | custom-call | tf_op jit(solution)/shard_map/pack_keys/pallas_call | solution.py:589
  2.5 8.6 %all-to-all-start.1 = ((bf16[32,80,128]{2,1,0:T(8,128)(2,1)}), bf16[32,80,128]{2,1,0:T(8,128)(2,1)S(1)}, u32[]{:S(2)}, u32[]{:S(2)}) async-start(bf16[32,80,128]{2,1,0:T(8,128)(2,1)} %pack_keys.1), calls=%async_computation.1 | async-start | bytes 1310720 | tf_op jit(solution)/shard_map/all_to_all | solution.py:700
  11.1 2.4 %pack_others.1 = bf16[32,192,128]{2,1,0:T(8,128)(2,1)} custom-call(bf16[64,2048]{1,0:T(8,128)(2,1)} %query_ref.1, bf16[64,4096]{1,0:T(8,128)(2,1)} %value_ref.1, bf16[64,4096]{1,0:T(8,128)(2,1)} %grad_ref.1), custom_call_target="tpu_custom_call" | custom-call | flops 1610612736 | bytes 1048576 | tf_op jit(solution)/shard_map/pack_others/pallas_call | solution.py:606
  13.6 10.5 %all-to-all-done.1.x_ref.keys_got_ref = bf16[32,80,128]{2,1,0:T(8,128)(2,1)S(1)} async-done(((bf16[32,80,128]{2,1,0:T(8,128)(2,1)}), bf16[32,80,128]{2,1,0:T(8,128)(2,1)S(1)}, u32[]{:S(2)}, u32[]{:S(2)}) %all-to-all-start.1) | async-done | bytes 655392 | tf_op jit(solution)/shard_map/all_to_all | solution.py:700
  24.1 0.8 copy-done.3
  24.9 3.8 %all-to-all-start = ((bf16[32,192,128]{2,1,0:T(8,128)(2,1)}), bf16[32,192,128]{2,1,0:T(8,128)(2,1)S(1)}, u32[]{:S(2)}, u32[]{:S(2)}) async-start(bf16[32,192,128]{2,1,0:T(8,128)(2,1)} %pack_others.1), calls=%async_computation | async-start | bytes 3145728 | tf_op jit(solution)/shard_map/all_to_all | solution.py:700
  28.7 0.6 dynamic_slice.8
  29.3 0.6 dynamic_slice.7
  29.9 0.6 slice_reduce_fusion
  30.5 0.6 slice_reduce_fusion.1
  31.1 1.9 %stack.25.ints_ref = s32[6]{0:T(128)} concatenate(s32[1]{0:T(128)} %bitcast, s32[1]{0:T(128)} %constant.26.clone.1, s32[1]{0:T(128)S(1)} %bitcast.11, s32[1]{0:T(128)} %bitcast.1, s32[1]{0:T(128)} %bitcast.2, s32[1]{0:T(128)} %bitcast.3), dimensions={0} | concatenate | bytes 48 | tf_op jit(solution)/shard_map/stack | solution.py:691
  33.0 1.9 %pad_maximum_fusion.floats_ref = f32[2]{0:T(128)} fusion(f32[1]{0:T(128)} %dynamic_slice.8, f32[1]{0:T(128)} %dynamic_slice.7), kind=kLoop, calls=%fused_computation | loop fusion | flops 2 | bytes 16 | tf_op jit(solution)/shard_map/stack | solution.py:692
  34.9 8.8 %maps.1 = (f32[4,16,128]{2,1,0:T(8,128)}, f32[2,128,128]{2,1,0:T(8,128)}, bf16[16,128,128]{2,1,0:T(8,128)(2,1)}, bf16[16,128,128]{2,1,0:T(8,128)(2,1)}, bf16[16,...) custom-call(s32[6]{0:T(128)} %stack.25.ints_ref, ...), custom_call_target="tpu_custom_call" | custom-call | flops 10737418240 | bytes 1048576 | tf_op jit(solution)/shard_map/maps/pallas_call | solution.py:217
  43.7 5.6 %collective-permute-start.6 = (bf16[128,128]{1,0:T(8,128)(2,1)}, bf16[128,128]{1,0:T(8,128)(2,1)S(1)}, u32[]{:S(2)}, u32[]{:S(2)}) collective-permute-start(bf16[128,128]{1,0:T(8,128)(2,1)} %get-tuple-element.44), channel_id=1, source_target_pairs={{0,224},{32,0},{64,32},{96,64},{128,96},{160,128},{192,160},{224,1... | collective-permute-start | bytes 98312 | tf_op jit(solution)/shard_map/ppermute | solution.py:672
  49.3 1.2 collective-permute-start.5
  50.5 0.5 collective-permute-start.4
  50.9 4.5 %collective-permute-start.3 = (bf16[128,128]{1,0:T(8,128)(2,1)}, bf16[128,128]{1,0:T(8,128)(2,1)S(1)}, u32[]{:S(2)}, u32[]{:S(2)}) collective-permute-start(bf16[128,128]{1,0:T(8,128)(2,1)} %get-tuple-element.44), channel_id=1, source_target_pairs={{0,128},{32,160},{64,192},{96,224},{128,0},{160,32},{192,64},{224,... | collective-permute-start | bytes 98312 | tf_op jit(solution)/shard_map/ppermute | solution.py:672
  55.4 2.1 %collective-permute-start.1 = (bf16[128,128]{1,0:T(8,128)(2,1)}, bf16[128,128]{1,0:T(8,128)(2,1)S(1)}, u32[]{:S(2)}, u32[]{:S(2)}) collective-permute-start(bf16[128,128]{1,0:T(8,128)(2,1)} %get-tuple-element.44), channel_id=1, source_target_pairs={{0,64},{32,96},{64,128},{96,160},{128,192},{160,224},{192,0},{224,... | collective-permute-start | bytes 98312 | tf_op jit(solution)/shard_map/ppermute | solution.py:672
  57.6 1.4 collective-permute-start
  59.0 0.0 collective-permute-done.4.refs_4_
  59.0 0.0 collective-permute-done.3.refs_3_
  59.0 2.4 %collective-permute-done.2.refs_2_ = bf16[128,128]{1,0:T(8,128)(2,1)S(1)} collective-permute-done((bf16[128,128]{1,0:T(8,128)(2,1)}, bf16[128,128]{1,0:T(8,128)(2,1)S(1)}, u32[]{:S(2)}, u32[]{:S(2)}) %collective-permute-start.2) | collective-permute-done | bytes 32800 | tf_op jit(solution)/shard_map/ppermute | solution.py:672
  61.4 0.6 collective-permute-done.1.refs_1_
  62.1 0.0 collective-permute-done.refs_0_
  62.1 0.6 copy-done.17
  62.7 0.6 copy-done.18
  63.3 2.5 %compose.1 = (bf16[128,896]{1,0:T(8,128)(2,1)}, bf16[128,896]{1,0:T(8,128)(2,1)}) custom-call(s32[6]{0:T(128)} %stack.25.ints_ref, bf16[128,128]{1,0:T(8,128)(2,1)} %copy-done.18, bf16[128,128]{1,0:T(8,128)(2,1)} %copy-done.17, bf16[128,128]{1,0:T(8,128)(2,1)} %copy-done.16, bf16[128,128]{1,0:T(8,128)(2,1)} %copy-done.15, bf16[128,128]{1,0:T(8,128)(2,1)} %copy-done.14, ...), custom_call_target="tpu_custom_call" | custom-call | flops 1073741824 | bytes 1048576 | tf_op jit(solution)/shard_map/compose/pallas_call | solution.py:252
  65.8 1.2 copy-done.1
  66.9 9.8 %states.1 = (bf16[16,128,128]{2,1,0:T(8,128)(2,1)}, bf16[16,128,128]{2,1,0:T(8,128)(2,1)}, bf16[16,128,128]{2,1,0:T(8,128)(2,1)}, bf16[16,128,128]{2,1,0:T(8,128...) custom-call(s32[6]{0:T(128)} %stack.25.ints_ref, ...), custom_call_target="tpu_custom_call" | custom-call | flops 7516192768 | bytes 1048576 | tf_op jit(solution)/shard_map/states/pallas_call | solution.py:350
  76.8 0.3 collective-permute-start.7
  77.1 2.6 %collective-permute-start.8 = (bf16[128,128]{1,0:T(8,128)(2,1)}, bf16[128,128]{1,0:T(8,128)(2,1)S(1)}, u32[]{:S(2)}, u32[]{:S(2)}) collective-permute-start(bf16[128,128]{1,0:T(8,128)(2,1)} %get-tuple-element.66), channel_id=1, source_target_pairs={{0,64},{32,96},{64,128},{96,160},{128,192},{160,224},{192,0},{224,... | collective-permute-start | bytes 98312 | tf_op jit(solution)/shard_map/ppermute | solution.py:672
  79.7 2.2 %collective-permute-start.9 = (bf16[128,128]{1,0:T(8,128)(2,1)}, bf16[128,128]{1,0:T(8,128)(2,1)S(1)}, u32[]{:S(2)}, u32[]{:S(2)}) collective-permute-start(bf16[128,128]{1,0:T(8,128)(2,1)} %get-tuple-element.67), channel_id=1, source_target_pairs={{0,96},{32,128},{64,160},{96,192},{128,224},{160,0},{192,32},{224,... | collective-permute-start | bytes 98312 | tf_op jit(solution)/shard_map/ppermute | solution.py:672
  81.9 2.0 %collective-permute-start.10 = (bf16[128,128]{1,0:T(8,128)(2,1)}, bf16[128,128]{1,0:T(8,128)(2,1)S(1)}, u32[]{:S(2)}, u32[]{:S(2)}) collective-permute-start(bf16[128,128]{1,0:T(8,128)(2,1)} %get-tuple-element.68), channel_id=1, source_target_pairs={{0,128},{32,160},{64,192},{96,224},{128,0},{160,32},{192,64},{224,... | collective-permute-start | bytes 98312 | tf_op jit(solution)/shard_map/ppermute | solution.py:672
  83.9 2.4 %collective-permute-start.11 = (bf16[128,128]{1,0:T(8,128)(2,1)}, bf16[128,128]{1,0:T(8,128)(2,1)S(1)}, u32[]{:S(2)}, u32[]{:S(2)}) collective-permute-start(bf16[128,128]{1,0:T(8,128)(2,1)} %get-tuple-element.69), channel_id=1, source_target_pairs={{0,160},{32,192},{64,224},{96,0},{128,32},{160,64},{192,96},{224,1... | collective-permute-start | bytes 98312 | tf_op jit(solution)/shard_map/ppermute | solution.py:672
  86.3 3.6 %collective-permute-start.12 = (bf16[128,128]{1,0:T(8,128)(2,1)}, bf16[128,128]{1,0:T(8,128)(2,1)S(1)}, u32[]{:S(2)}, u32[]{:S(2)}) collective-permute-start(bf16[128,128]{1,0:T(8,128)(2,1)} %get-tuple-element.70), channel_id=1, source_target_pairs={{0,192},{32,224},{64,0},{96,32},{128,64},{160,96},{192,128},{224,1... | collective-permute-start | bytes 98312 | tf_op jit(solution)/shard_map/ppermute | solution.py:672
  89.9 0.5 collective-permute-start.13
  90.4 0.8 collective-permute-done.12.rest_5_
  91.2 3.4 %collective-permute-done.13.rest_6_ = bf16[128,128]{1,0:T(8,128)(2,1)S(1)} collective-permute-done((bf16[128,128]{1,0:T(8,128)(2,1)}, bf16[128,128]{1,0:T(8,128)(2,1)S(1)}, u32[]{:S(2)}, u32[]{:S(2)}) %collective-permute-start.13) | collective-permute-done | bytes 32800 | tf_op jit(solution)/shard_map/ppermute | solution.py:672
  94.6 0.6 copy-done.13
  95.2 4.6 %outputs.1 = (bf16[32,128,128]{2,1,0:T(8,128)(2,1)}, bf16[16,128,128]{2,1,0:T(8,128)(2,1)}, bf16[16,128,128]{2,1,0:T(8,128)(2,1)}, bf16[16,128,128]{2,1,0:T(8,128)(2,1)}) custom-call(bf16[128,896]{1,0:T(8,128)(2,1)} %get-tuple-element.47.forward_ref, bf16[128,896]{1,0:T(8,128)(2,1)} %get-tuple-element.48.backward_ref, ...), custom_call_target="tpu_custom_call" | custom-call | flops 2684354560 | bytes 1048576 | tf_op jit(solution)/shard_map/outputs/pallas_call | solution.py:424
  99.8 10.2 %all-to-all-start.2 = ((bf16[32,128,128]{2,1,0:T(8,128)(2,1)}), bf16[32,128,128]{2,1,0:T(8,128)(2,1)S(1)}, u32[]{:S(2)}, u32[]{:S(2)}) async-start(bf16[32,128,128]{2,1,0:T(8,128)(2,1)} %get-tuple-element.72.y_ref), calls=%async_computation.2 | async-start | bytes 2097152 | tf_op jit(solution)/shard_map/all_to_all | solution.py:700
  109.9 7.8 %gradients.1 = bf16[32,144,128]{2,1,0:T(8,128)(2,1)} custom-call(s32[6]{0:T(128)} %stack.25.ints_ref, bf16[32,80,128]{2,1,0:T(8,128)(2,1)} %copy-done.3, bf16[32,192,128]{2,1,0:T(8,128)(2,1)} %copy-done.1, f32[4,16,128]{2,1,0:T(8,128)} %get-tuple-element.54.gate_ref, f32[2,128,128]{2,1,0:T(8,128)} %get-tuple-element.55.column_ref, ...), custom_call_target="tpu_custom_call" | custom-call | flops 7516192768 | bytes 1048576 | tf_op jit(solution)/shard_map/gradients/pallas_call | solution.py:538
  117.7 9.1 %all-to-all-done.2.y_ref = bf16[32,128,128]{2,1,0:T(8,128)(2,1)S(1)} async-done(((bf16[32,128,128]{2,1,0:T(8,128)(2,1)}), bf16[32,128,128]{2,1,0:T(8,128)(2,1)S(1)}, u32[]{:S(2)}, u32[]{:S(2)}) %all-to-all-start.2) | async-done | bytes 1048608 | tf_op jit(solution)/shard_map/all_to_all | solution.py:700
  126.8 4.0 %all-to-all-start.3 = ((bf16[32,144,128]{2,1,0:T(8,128)(2,1)}), bf16[32,144,128]{2,1,0:T(8,128)(2,1)S(1)}, u32[]{:S(2)}, u32[]{:S(2)}) async-start(bf16[32,144,128]{2,1,0:T(8,128)(2,1)} %gradients.1), calls=%async_computation.3 | async-start | bytes 2359296 | tf_op jit(solution)/shard_map/all_to_all | solution.py:700
  130.8 2.2 %unpack_outputs.1 = (bf16[64,4096]{1,0:T(8,128)(2,1)}, bf16[64,4096]{1,0:T(8,128)(2,1)}) custom-call(bf16[32,128,128]{2,1,0:T(8,128)(2,1)} %copy-done.2), custom_call_target="tpu_custom_call" | custom-call | flops 1610612736 | bytes 1048576 | tf_op jit(solution)/shard_map/unpack_outputs/pallas_call | solution.py:627
  133.0 16.2 %all-to-all-done.3.z_ref = bf16[32,144,128]{2,1,0:T(8,128)(2,1)S(1)} async-done(((bf16[32,144,128]{2,1,0:T(8,128)(2,1)}), bf16[32,144,128]{2,1,0:T(8,128)(2,1)S(1)}, u32[]{:S(2)}, u32[]{:S(2)}) %all-to-all-start.3) | async-done | bytes 1179680 | tf_op jit(solution)/shard_map/all_to_all | solution.py:700
  149.2 1.0 copy-done
  150.2 2.1 %unpack_gradients.1 = (bf16[64,2048]{1,0:T(8,128)(2,1)}, bf16[64,2048]{1,0:T(8,128)(2,1)}, bf16[32,64]{1,0:T(8,128)(2,1)}, bf16[32,64]{1,0:T(8,128)(2,1)}) custom-call(s32[6]{0:T(128)} %stack.25.ints_ref, bf16[32,144,128]{2,1,0:T(8,128)(2,1)} %copy-done), custom_call_target="tpu_custom_call" | custom-call | tf_op jit(solution)/shard_map/unpack_gradients/pallas_call | solution.py:656
  (45 shorter events, 0.1 us)
Async XLA Ops:
  2.5 21.5 %all-to-all-start.1 = ((bf16[32,80,128]{2,1,0:T(8,128)(2,1)}), bf16[32,80,128]{2,1,0:T(8,128)(2,1)S(1)}, u32[]{:S(2)}, u32[]{:S(2)}) async-start(bf16[32,80,128]{2,1,0:T(8,128)(2,1)} %pack_keys.1), calls=%async_computation.1 | async-start | bytes 1310720 | tf_op jit(solution)/shard_map/all_to_all | solution.py:700
  13.6 15.1 %copy-start.19 = (f32[32]{0:T(128)S(1)}, f32[32]{0:T(128)}, u32[]{:S(2)}) copy-start(f32[32]{0:T(128)} %param.15) | copy-start | bytes 388
  13.6 15.7 %copy-start.20 = (f32[32]{0:T(128)S(1)}, f32[32]{0:T(128)}, u32[]{:S(2)}) copy-start(f32[32]{0:T(128)} %param.14) | copy-start | bytes 388
  13.6 16.3 %copy-start.4 = (s32[4]{0:T(128)S(1)}, s32[4]{0:T(128)}, u32[]{:S(2)}) copy-start(s32[4]{0:T(128)} %param.16) | copy-start | bytes 52
  24.1 0.8 copy-start.3
  24.9 40.8 %all-to-all-start = ((bf16[32,192,128]{2,1,0:T(8,128)(2,1)}), bf16[32,192,128]{2,1,0:T(8,128)(2,1)S(1)}, u32[]{:S(2)}, u32[]{:S(2)}) async-start(bf16[32,192,128]{2,1,0:T(8,128)(2,1)} %pack_others.1), calls=%async_computation | async-start | bytes 3145728 | tf_op jit(solution)/shard_map/all_to_all | solution.py:700
  43.7 11.7 %collective-permute-start.6 = (bf16[128,128]{1,0:T(8,128)(2,1)}, bf16[128,128]{1,0:T(8,128)(2,1)S(1)}, u32[]{:S(2)}, u32[]{:S(2)}) collective-permute-start(bf16[128,128]{1,0:T(8,128)(2,1)} %get-tuple-element.44), channel_id=1, source_target_pairs={{0,224},{32,0},{64,32},{96,64},{128,96},{160,128},{192,160},{224,1... | collective-permute-start | bytes 98312 | tf_op jit(solution)/shard_map/ppermute | solution.py:672
  49.3 8.3 %collective-permute-start.5 = (bf16[128,128]{1,0:T(8,128)(2,1)}, bf16[128,128]{1,0:T(8,128)(2,1)S(1)}, u32[]{:S(2)}, u32[]{:S(2)}) collective-permute-start(bf16[128,128]{1,0:T(8,128)(2,1)} %get-tuple-element.44), channel_id=1, source_target_pairs={{0,192},{32,224},{64,0},{96,32},{128,64},{160,96},{192,128},{224,1... | collective-permute-start | bytes 98312 | tf_op jit(solution)/shard_map/ppermute | solution.py:672
  50.5 8.5 %collective-permute-start.4 = (bf16[128,128]{1,0:T(8,128)(2,1)}, bf16[128,128]{1,0:T(8,128)(2,1)S(1)}, u32[]{:S(2)}, u32[]{:S(2)}) collective-permute-start(bf16[128,128]{1,0:T(8,128)(2,1)} %get-tuple-element.44), channel_id=1, source_target_pairs={{0,160},{32,192},{64,224},{96,0},{128,32},{160,64},{192,96},{224,1... | collective-permute-start | bytes 98312 | tf_op jit(solution)/shard_map/ppermute | solution.py:672
  50.9 8.0 %collective-permute-start.3 = (bf16[128,128]{1,0:T(8,128)(2,1)}, bf16[128,128]{1,0:T(8,128)(2,1)S(1)}, u32[]{:S(2)}, u32[]{:S(2)}) collective-permute-start(bf16[128,128]{1,0:T(8,128)(2,1)} %get-tuple-element.44), channel_id=1, source_target_pairs={{0,128},{32,160},{64,192},{96,224},{128,0},{160,32},{192,64},{224,... | collective-permute-start | bytes 98312 | tf_op jit(solution)/shard_map/ppermute | solution.py:672
  55.4 6.0 %collective-permute-start.2 = (bf16[128,128]{1,0:T(8,128)(2,1)}, bf16[128,128]{1,0:T(8,128)(2,1)S(1)}, u32[]{:S(2)}, u32[]{:S(2)}) collective-permute-start(bf16[128,128]{1,0:T(8,128)(2,1)} %get-tuple-element.44), channel_id=1, source_target_pairs={{0,96},{32,128},{64,160},{96,192},{128,224},{160,0},{192,32},{224,... | collective-permute-start | bytes 98312 | tf_op jit(solution)/shard_map/ppermute | solution.py:672
  55.4 6.6 %copy-start.11 = (bf16[128,128]{1,0:T(8,128)(2,1)}, bf16[128,128]{1,0:T(8,128)(2,1)S(1)}, u32[]{:S(2)}) copy-start(bf16[128,128]{1,0:T(8,128)(2,1)S(1)} %collective-permute-done.6.refs_6_) | copy-start | bytes 98308
  55.4 6.6 %collective-permute-start.1 = (bf16[128,128]{1,0:T(8,128)(2,1)}, bf16[128,128]{1,0:T(8,128)(2,1)S(1)}, u32[]{:S(2)}, u32[]{:S(2)}) collective-permute-start(bf16[128,128]{1,0:T(8,128)(2,1)} %get-tuple-element.44), channel_id=1, source_target_pairs={{0,64},{32,96},{64,128},{96,160},{128,192},{160,224},{192,0},{224,... | collective-permute-start | bytes 98312 | tf_op jit(solution)/shard_map/ppermute | solution.py:672
  57.6 4.5 %copy-start.12 = (bf16[128,128]{1,0:T(8,128)(2,1)}, bf16[128,128]{1,0:T(8,128)(2,1)S(1)}, u32[]{:S(2)}) copy-start(bf16[128,128]{1,0:T(8,128)(2,1)S(1)} %collective-permute-done.5.refs_5_) | copy-start | bytes 98308
  57.6 4.5 %collective-permute-start = (bf16[128,128]{1,0:T(8,128)(2,1)}, bf16[128,128]{1,0:T(8,128)(2,1)S(1)}, u32[]{:S(2)}, u32[]{:S(2)}) collective-permute-start(bf16[128,128]{1,0:T(8,128)(2,1)} %get-tuple-element.44), channel_id=1, source_target_pairs={{0,32},{32,64},{64,96},{96,128},{128,160},{160,192},{192,224},{224... | collective-permute-start | bytes 98312 | tf_op jit(solution)/shard_map/ppermute | solution.py:672
  59.0 3.1 %copy-start.14 = (bf16[128,128]{1,0:T(8,128)(2,1)}, bf16[128,128]{1,0:T(8,128)(2,1)S(1)}, u32[]{:S(2)}) copy-start(bf16[128,128]{1,0:T(8,128)(2,1)S(1)} %collective-permute-done.4.refs_4_) | copy-start | bytes 98308
  59.0 3.1 %copy-start.15 = (bf16[128,128]{1,0:T(8,128)(2,1)}, bf16[128,128]{1,0:T(8,128)(2,1)S(1)}, u32[]{:S(2)}) copy-start(bf16[128,128]{1,0:T(8,128)(2,1)S(1)} %collective-permute-done.3.refs_3_) | copy-start | bytes 98308
  61.4 0.7 copy-start.16
  62.1 0.6 copy-start.17
  62.7 0.6 copy-start.18
  65.8 1.2 copy-start.1
  76.8 9.6 %collective-permute-start.7 = (bf16[128,128]{1,0:T(8,128)(2,1)}, bf16[128,128]{1,0:T(8,128)(2,1)S(1)}, u32[]{:S(2)}, u32[]{:S(2)}) collective-permute-start(bf16[128,128]{1,0:T(8,128)(2,1)} %get-tuple-element.65), channel_id=1, source_target_pairs={{0,32},{32,64},{64,96},{96,128},{128,160},{160,192},{192,224},{224... | collective-permute-start | bytes 98312 | tf_op jit(solution)/shard_map/ppermute | solution.py:672
  77.1 12.8 %collective-permute-start.8 = (bf16[128,128]{1,0:T(8,128)(2,1)}, bf16[128,128]{1,0:T(8,128)(2,1)S(1)}, u32[]{:S(2)}, u32[]{:S(2)}) collective-permute-start(bf16[128,128]{1,0:T(8,128)(2,1)} %get-tuple-element.66), channel_id=1, source_target_pairs={{0,64},{32,96},{64,128},{96,160},{128,192},{160,224},{192,0},{224,... | collective-permute-start | bytes 98312 | tf_op jit(solution)/shard_map/ppermute | solution.py:672
  79.7 10.6 %collective-permute-start.9 = (bf16[128,128]{1,0:T(8,128)(2,1)}, bf16[128,128]{1,0:T(8,128)(2,1)S(1)}, u32[]{:S(2)}, u32[]{:S(2)}) collective-permute-start(bf16[128,128]{1,0:T(8,128)(2,1)} %get-tuple-element.67), channel_id=1, source_target_pairs={{0,96},{32,128},{64,160},{96,192},{128,224},{160,0},{192,32},{224,... | collective-permute-start | bytes 98312 | tf_op jit(solution)/shard_map/ppermute | solution.py:672
  81.9 8.5 %collective-permute-start.10 = (bf16[128,128]{1,0:T(8,128)(2,1)}, bf16[128,128]{1,0:T(8,128)(2,1)S(1)}, u32[]{:S(2)}, u32[]{:S(2)}) collective-permute-start(bf16[128,128]{1,0:T(8,128)(2,1)} %get-tuple-element.68), channel_id=1, source_target_pairs={{0,128},{32,160},{64,192},{96,224},{128,0},{160,32},{192,64},{224,... | collective-permute-start | bytes 98312 | tf_op jit(solution)/shard_map/ppermute | solution.py:672
  83.9 6.5 %collective-permute-start.11 = (bf16[128,128]{1,0:T(8,128)(2,1)}, bf16[128,128]{1,0:T(8,128)(2,1)S(1)}, u32[]{:S(2)}, u32[]{:S(2)}) collective-permute-start(bf16[128,128]{1,0:T(8,128)(2,1)} %get-tuple-element.69), channel_id=1, source_target_pairs={{0,160},{32,192},{64,224},{96,0},{128,32},{160,64},{192,96},{224,1... | collective-permute-start | bytes 98312 | tf_op jit(solution)/shard_map/ppermute | solution.py:672
  86.3 8.3 %copy-start.5 = (bf16[128,128]{1,0:T(8,128)(2,1)}, bf16[128,128]{1,0:T(8,128)(2,1)S(1)}, u32[]{:S(2)}) copy-start(bf16[128,128]{1,0:T(8,128)(2,1)S(1)} %collective-permute-done.7.rest_0_) | copy-start | bytes 98308
  86.3 4.9 %collective-permute-start.12 = (bf16[128,128]{1,0:T(8,128)(2,1)}, bf16[128,128]{1,0:T(8,128)(2,1)S(1)}, u32[]{:S(2)}, u32[]{:S(2)}) collective-permute-start(bf16[128,128]{1,0:T(8,128)(2,1)} %get-tuple-element.70), channel_id=1, source_target_pairs={{0,192},{32,224},{64,0},{96,32},{128,64},{160,96},{192,128},{224,1... | collective-permute-start | bytes 98312 | tf_op jit(solution)/shard_map/ppermute | solution.py:672
  89.9 4.7 %copy-start.6 = (bf16[128,128]{1,0:T(8,128)(2,1)}, bf16[128,128]{1,0:T(8,128)(2,1)S(1)}, u32[]{:S(2)}) copy-start(bf16[128,128]{1,0:T(8,128)(2,1)S(1)} %collective-permute-done.8.rest_1_) | copy-start | bytes 98308
  89.9 4.7 %collective-permute-start.13 = (bf16[128,128]{1,0:T(8,128)(2,1)}, bf16[128,128]{1,0:T(8,128)(2,1)S(1)}, u32[]{:S(2)}, u32[]{:S(2)}) collective-permute-start(bf16[128,128]{1,0:T(8,128)(2,1)} %get-tuple-element.71), channel_id=1, source_target_pairs={{0,224},{32,0},{64,32},{96,64},{128,96},{160,128},{192,160},{224,1... | collective-permute-start | bytes 98312 | tf_op jit(solution)/shard_map/ppermute | solution.py:672
  90.4 4.2 %copy-start.7 = (bf16[128,128]{1,0:T(8,128)(2,1)}, bf16[128,128]{1,0:T(8,128)(2,1)S(1)}, u32[]{:S(2)}) copy-start(bf16[128,128]{1,0:T(8,128)(2,1)S(1)} %collective-permute-done.9.rest_2_) | copy-start | bytes 98308
  90.4 4.2 %copy-start.8 = (bf16[128,128]{1,0:T(8,128)(2,1)}, bf16[128,128]{1,0:T(8,128)(2,1)S(1)}, u32[]{:S(2)}) copy-start(bf16[128,128]{1,0:T(8,128)(2,1)S(1)} %collective-permute-done.10.rest_3_) | copy-start | bytes 98308
  90.4 4.2 %copy-start.9 = (bf16[128,128]{1,0:T(8,128)(2,1)}, bf16[128,128]{1,0:T(8,128)(2,1)S(1)}, u32[]{:S(2)}) copy-start(bf16[128,128]{1,0:T(8,128)(2,1)S(1)} %collective-permute-done.11.rest_4_) | copy-start | bytes 98308
  91.2 3.4 %copy-start.10 = (bf16[128,128]{1,0:T(8,128)(2,1)}, bf16[128,128]{1,0:T(8,128)(2,1)S(1)}, u32[]{:S(2)}) copy-start(bf16[128,128]{1,0:T(8,128)(2,1)S(1)} %collective-permute-done.12.rest_5_) | copy-start | bytes 98308
  94.6 0.6 copy-start.13
  99.8 27.1 %all-to-all-start.2 = ((bf16[32,128,128]{2,1,0:T(8,128)(2,1)}), bf16[32,128,128]{2,1,0:T(8,128)(2,1)S(1)}, u32[]{:S(2)}, u32[]{:S(2)}) async-start(bf16[32,128,128]{2,1,0:T(8,128)(2,1)} %get-tuple-element.72.y_ref), calls=%async_computation.2 | async-start | bytes 2097152 | tf_op jit(solution)/shard_map/all_to_all | solution.py:700
  126.8 4.0 %copy-start.2 = (bf16[32,128,128]{2,1,0:T(8,128)(2,1)}, bf16[32,128,128]{2,1,0:T(8,128)(2,1)S(1)}, u32[]{:S(2)}) copy-start(bf16[32,128,128]{2,1,0:T(8,128)(2,1)S(1)} %all-to-all-done.2.y_ref) | copy-start | bytes 3145732
  126.8 22.3 %all-to-all-start.3 = ((bf16[32,144,128]{2,1,0:T(8,128)(2,1)}), bf16[32,144,128]{2,1,0:T(8,128)(2,1)S(1)}, u32[]{:S(2)}, u32[]{:S(2)}) async-start(bf16[32,144,128]{2,1,0:T(8,128)(2,1)} %gradients.1), calls=%async_computation.3 | async-start | bytes 2359296 | tf_op jit(solution)/shard_map/all_to_all | solution.py:700
  149.2 1.0 copy-start

commit v2 on v0

v2 whole, which is shorter than its diff:
```python
import functools

import jax
import jax.numpy as jnp
from jax import lax
from jax.experimental import pallas as pl
from jax.experimental.pallas import tpu as pltpu
from jax.sharding import PartitionSpec as P

VALUE_HEAD_COUNT = 32
NK = 16
DK = 128
DV = 128
GROUP = 128
GATE_ROWS = 16
PACK_HEADS = 16
BLOCKS = 16
SHARDS = 8
GRADIENT_BLOCKS = 4
LATER_BLOCKS = 8
SMALL_VMEM = 24 * 1024 * 1024
LARGE_VMEM = 58 * 1024 * 1024

bf16 = jnp.bfloat16
f32 = jnp.float32


def contract(left, right, left_dim, right_dim):
    return lax.dot_general(
        left.astype(bf16),
        right.astype(bf16),
        (((left_dim,), (right_dim,)), ((), ())),
        preferred_element_type=f32,
    )


def mm(left, right):
    return contract(left, right, 1, 0)


def mm_nt(left, right):
    return contract(left, right, 1, 1)


def mm_tn(left, right):
    return contract(left, right, 0, 0)


def exact(left, right, left_dim, right_dim):
    return lax.dot_general(
        left,
        right,
        (((left_dim,), (right_dim,)), ((), ())),
        preferred_element_type=f32,
        precision=lax.Precision.HIGHEST,
    )


def iota(shape, dim):
    return lax.broadcasted_iota(jnp.int32, shape, dim)


def segment_of(positions, starts):
    count = jnp.zeros(positions.shape, jnp.int32)
    for start in starts:
        count = count + jnp.where(positions >= start, 1, 0)
    return count


def pick_column(table, block):
    lane = iota(table.shape, 1)
    return jnp.sum(jnp.where(lane == block, table, 0.0), axis=1, keepdims=True)


def block_gates(block, ints_ref, gate_ref, column_ref):
    starts = [ints_ref[1 + j] for j in range(4)]
    first = ints_ref[0] * 16 * GROUP + block * GROUP
    cum_row = gate_ref[0, pl.ds(block, 1), :]
    beta_row = gate_ref[1, pl.ds(block, 1), :]
    cum_col = pick_column(column_ref[0], block)
    beta_col = pick_column(column_ref[1], block)
    seg_row = segment_of(first + iota((1, GROUP), 1), starts)
    seg_col = segment_of(first + iota((GROUP, 1), 0), starts)
    before = segment_of(jnp.full((1, 1), first - 1, jnp.int32), starts)
    row, col = iota((GROUP, GROUP), 0), iota((GROUP, GROUP), 1)
    joined = (row >= col) & (seg_col == seg_row)
    spread = jnp.where(joined, cum_col - cum_row, 0.0)
    weighted = jnp.where(joined, jnp.exp(spread), 0.0) * beta_row
    entry = jnp.where(seg_col == before, jnp.exp(cum_col), 0.0)
    cum_last = cum_col[GROUP - 1 :, :]
    same_last = seg_col == seg_col[GROUP - 1 :, :]
    last = (
        jnp.where(same_last, jnp.exp(jnp.where(same_last, cum_last - cum_col, 0.0)), 0.0) * beta_col
    )
    return weighted, entry, last


def inverse_root(raw):
    return lax.rsqrt(jnp.sum(raw * raw, axis=1, keepdims=True) + 1e-06)


def block_rows(x_ref, local, part):
    return jnp.concatenate(
        [x_ref[2 * local + half, 64 * part : 64 * part + 64, :] for half in range(2)], axis=0
    )


def normed(x_ref, local):
    query_raw = block_rows(x_ref, local, 0).astype(f32)
    key_raw = block_rows(x_ref, local, 1).astype(f32)
    query_root, key_root = inverse_root(query_raw), inverse_root(key_raw)
    query = query_raw * query_root * DK ** (-0.5)
    keys = key_raw * key_root
    return query_raw, key_raw, query_root, key_root, query.astype(bf16), keys.astype(bf16)


def eye_of(size):
    return jnp.where(iota((size, size), 0) == iota((size, size), 1), 1.0, 0.0)


def cost(units):
    return pl.CostEstimate(
        flops=units * BLOCKS * 2 * 128**3 * 8, bytes_accessed=1 << 20, transcendentals=0
    )


def whole(*shape):
    return pl.BlockSpec(shape, lambda i: (0,) * len(shape))


def stepped(count, *shape):
    return pl.BlockSpec((count, *shape), lambda i: (i,) + (0,) * len(shape))


def triangular_inverses(stricts, row, col):
    differ = row ^ col
    eye = jnp.where(differ == 0, 1.0, 0.0)
    inverses = [eye - jnp.where(differ == 1, strict, 0.0) for strict in stricts]
    for level in range(1, 7):
        size = 1 << level
        band = (differ >= size) & (differ < 2 * size)
        held = [inverse.astype(bf16) for inverse in inverses]
        half = [
            mm(one, jnp.where(band, strict, 0.0)) for one, strict in zip(held, stricts)
        ]
        step = [mm(one, other) for one, other in zip(half, held)]
        inverses = [inverse - one for inverse, one in zip(inverses, step)]
    held = [inverse.astype(bf16) for inverse in inverses]
    upper = [strict.astype(bf16) for strict in stricts]
    lower = [(strict - one.astype(f32)).astype(bf16) for strict, one in zip(stricts, upper)]
    rest = [mm(one, other) for one, other in zip(upper, held)]
    fine = [mm(one, other) for one, other in zip(lower, held)]
    rest = [
        eye - one.astype(f32) - high - low for one, high, low in zip(held, rest, fine)
    ]
    return [one.astype(f32) + mm(one, other) for one, other in zip(held, rest)]


def tables_kernel(
    ints_ref,
    floats_ref,
    x_ref,
    send_ref,
    gate_ref,
    column_ref,
    inverse_ref,
    mixing_ref,
    keys_last_ref,
    fresh_ref,
    maps_ref,
    prefix_ref,
    prefix_free_ref,
    suffix_ref,
    suffix_free_ref,
):
    tail = x_ref[:, 256:, :].astype(f32)
    paired = tail.reshape(BLOCKS, 2, GATE_ROWS, 128)
    lane = iota((BLOCKS, GATE_ROWS, 128), 2)
    rows = iota((BLOCKS, GATE_ROWS, 128), 1)
    tail = jnp.where(lane < 64, paired[:, 0], paired[:, 1])
    decay_raw = jnp.sum(jnp.where(rows == 0, tail, 0.0), axis=1) + floats_ref[1]
    beta_raw = jnp.sum(jnp.where(rows == 1, tail, 0.0), axis=1)
    rate = -jnp.exp(jnp.full((BLOCKS, 128), floats_ref[0], f32))
    decay_log = rate * (jnp.maximum(decay_raw, 0.0) + jnp.log1p(jnp.exp(-jnp.abs(decay_raw))))
    row, col = iota((128, 128), 0), iota((128, 128), 1)
    eye = eye_of(128)
    cumulative = exact(decay_log, jnp.where(row <= col, 1.0, 0.0), 1, 0)
    beta = jax.nn.sigmoid(beta_raw)
    gate_ref[0] = cumulative
    gate_ref[1] = beta
    gate_ref[2] = rate * jax.nn.sigmoid(decay_raw)
    padding = jnp.zeros((128 - BLOCKS, 128), f32)
    column_ref[0] = exact(eye, jnp.concatenate([cumulative, padding], 0), 1, 1)
    column_ref[1] = exact(eye, jnp.concatenate([beta, padding], 0), 1, 1)

    each = range(BLOCKS)
    units = [normed(x_ref, i)[4:] for i in each]
    both = [mm_nt(jnp.concatenate([keys, query], 0), keys) for query, keys in units]
    gates = [block_gates(i, ints_ref, gate_ref, column_ref) for i in each]
    stricts = [jnp.where(row > col, gate[0] * one[:GROUP], 0.0) for gate, one in zip(gates, both)]
    mixing = [(gate[0] * one[GROUP:]).astype(bf16) for gate, one in zip(gates, both)]
    for i in each:
        mixing_ref[i] = mixing[i]
    inverses = [one.astype(bf16) for one in triangular_inverses(stricts, row, col)]
    keys_entry = [(units[i][1].astype(f32) * gates[i][1]).astype(bf16) for i in each]
    keys_last = [(units[i][1].astype(f32) * gates[i][2]).astype(bf16) for i in each]
    for i in each:
        inverse_ref[i] = inverses[i]
        keys_last_ref[i] = keys_last[i]
    pairs = [
        mm(inverses[i], jnp.concatenate([block_rows(x_ref, i, 2), keys_entry[i]], 1)).astype(bf16)
        for i in each
    ]
    seen = [pairs[i][:, DV:] for i in each]
    written = [mm_tn(keys_last[i], pairs[i]) for i in each]
    reads = [
        (gates[i][1] * units[i][0].astype(f32) - mm(mixing[i], seen[i])).astype(bf16) for i in each
    ]
    terms = [mm_tn(reads[i], block_rows(x_ref, i, 3)) for i in each]
    steps = [written[i][:, DV:].astype(bf16) for i in each]
    scales = [gates[i][1][GROUP - 1 :, :] for i in each]
    for i in each:
        fresh_ref[i] = pairs[i][:, :DV]
        maps_ref[i, 0] = seen[i]
        maps_ref[i, 1] = reads[i]
    nothing = jnp.zeros((DK, DK), f32)
    forward = jnp.concatenate([jnp.zeros((DK, DV), f32), eye], 1)
    backward = forward
    for i in each:
        other = BLOCKS - 1 - i
        forward_low, backward_low = forward.astype(bf16), backward.astype(bf16)
        prefix_free_ref[i] = forward_low[:, :DV]
        prefix_ref[i] = forward_low[:, DV:]
        suffix_free_ref[other] = backward_low[:, :DV]
        suffix_ref[other] = backward_low[:, DV:]
        forward = (
            scales[i] * forward
            - mm(steps[i], forward_low)
            + jnp.concatenate([written[i][:, :DV], nothing], 1)
        )
        backward = (
            scales[other] * backward
            - mm_tn(steps[other], backward_low)
            + jnp.concatenate([terms[other], nothing], 1)
        )
    total = forward[:, DV:].astype(bf16)
    for other in range(SHARDS):
        send_ref[other, :DK] = total
        send_ref[other, DK:] = jnp.where(
            ints_ref[0] < other, forward[:, :DV], backward[:, :DV]
        ).astype(bf16)


def tables(ints, floats, received):
    half = pltpu.HBM((BLOCKS, DK, DV), bf16)
    vmem = pl.BlockSpec(memory_space=pltpu.VMEM)
    smem = pl.BlockSpec(memory_space=pltpu.SMEM)
    return pl.pallas_call(
        tables_kernel,
        in_specs=[smem, smem, vmem],
        out_specs=[vmem] * 12,
        out_shape=[
            jax.ShapeDtypeStruct((SHARDS, 2 * DK, DV), bf16),
            pltpu.HBM((3, BLOCKS, 128), f32),
            pltpu.HBM((2, 128, 128), f32),
            *[half] * 4,
            pltpu.HBM((BLOCKS, 2, GROUP, DV), bf16),
            *[half] * 4,
        ],
        compiler_params=pltpu.CompilerParams(vmem_limit_bytes=SMALL_VMEM),
        cost_estimate=cost(30),
        name="tables",
    )(ints, floats, received)


def later_kernel(x_ref, inverse_ref, mixing_ref, keys_last_ref, fresh_ref, out_ref, push_ref, back_ref):
    each = range(LATER_BLOCKS)
    turned = [mm_tn(mixing_ref[i], block_rows(x_ref, i, 3)).astype(bf16) for i in each]
    outputs = [mm(mixing_ref[i], fresh_ref[i]) for i in each]
    pushed = [
        mm_tn(inverse_ref[i], jnp.concatenate([turned[i], keys_last_ref[i]], 1)).astype(bf16)
        for i in each
    ]
    for i in each:
        out_ref[i] = outputs[i].astype(bf16)
        push_ref[i] = pushed[i][:, :DV]
        back_ref[i] = pushed[i][:, DV:]


def later(received, inverse, mixing, keys_last, fresh):
    half = pltpu.HBM((BLOCKS, DK, DV), bf16)
    by_step = stepped(LATER_BLOCKS, GROUP, DV)
    return pl.pallas_call(
        later_kernel,
        grid=(BLOCKS // LATER_BLOCKS,),
        in_specs=[stepped(2 * LATER_BLOCKS, 256 + GATE_ROWS, 128)] + [by_step] * 4,
        out_specs=[by_step] * 3,
        out_shape=[half] * 3,
        compiler_params=pltpu.CompilerParams(vmem_limit_bytes=LARGE_VMEM),
        cost_estimate=cost(4),
        name="later",
    )(received, inverse, mixing, keys_last, fresh)


def split_two(state):
    high = state.astype(bf16)
    return jnp.concatenate([high, (state - high.astype(f32)).astype(bf16)], 1)


def gradients_kernel(
    ints_ref,
    x_ref,
    shards_ref,
    gate_ref,
    column_ref,
    out_ref,
    push_ref,
    back_ref,
    fresh_ref,
    maps_ref,
    prefix_ref,
    prefix_free_ref,
    suffix_ref,
    suffix_free_ref,
    y_ref,
    ends_ref,
):
    here = pl.program_id(0)

    @pl.when(here == 0)
    def prologue():
        me = ints_ref[0]
        state = jnp.zeros((DK, DV), f32)
        adjoint = jnp.zeros((DK, DV), f32)
        for k in range(7):
            moved = mm(shards_ref[k, :DK], split_two(state))
            new = moved[:, :DV] + moved[:, DV:] + shards_ref[k, DK:].astype(f32)
            state = jnp.where(k < me, new, state)
            at = 7 - k
            moved = mm_tn(shards_ref[at, :DK], split_two(adjoint))
            new = moved[:, :DV] + moved[:, DV:] + shards_ref[at, DK:].astype(f32)
            adjoint = jnp.where(at > me, new, adjoint)
        ends_ref[0] = state.astype(bf16)
        ends_ref[1] = adjoint.astype(bf16)

    lane = iota((GROUP, 8), 1)
    sublane = iota((8, GROUP), 0)
    change_cols = jnp.zeros((GROUP, 8), f32)
    beta_cols = jnp.zeros((GROUP, 8), f32)
    column_sums = jnp.zeros((8, GROUP), f32)
    each = range(GRADIENT_BLOCKS)
    row, col = iota((GROUP, GROUP), 0), iota((GROUP, GROUP), 1)
    states = [prefix_free_ref[i].astype(f32) + mm(prefix_ref[i], ends_ref[0]) for i in each]
    adjoints = [suffix_free_ref[i].astype(f32) + mm(suffix_ref[i], ends_ref[1]) for i in each]
    states_low = [one.astype(bf16) for one in states]
    adjoints_low = [one.astype(bf16) for one in adjoints]
    reads = [mm(maps_ref[i].reshape(2 * GROUP, DK), states_low[i]) for i in each]
    fresh = [(fresh_ref[i].astype(f32) - reads[i][:GROUP]).astype(bf16) for i in each]
    outputs = [out_ref[i].astype(f32) + reads[i][GROUP:] for i in each]
    pushed = [push_ref[i].astype(f32) + mm(back_ref[i], adjoints_low[i]) for i in each]
    norms = [normed(x_ref, i) for i in each]
    both = [mm_nt(jnp.concatenate([one[5], one[4]], 0), one[5]) for one in norms]
    sides = [
        jnp.concatenate([block_rows(x_ref, i, 3), pushed[i].astype(bf16)], 0) for i in each
    ]
    on_fresh = [mm_nt(sides[i], fresh[i]) for i in each]
    on_state = [mm_nt(sides[i], states_low[i]) for i in each]
    on_adjoint = [mm_nt(fresh[i], adjoints_low[i]) for i in each]
    gates = [
        block_gates(here * GRADIENT_BLOCKS + i, ints_ref, gate_ref, column_ref) for i in each
    ]
    mix_terms = [gates[i][0] * on_fresh[i][:GROUP] for i in each]
    key_terms = [jnp.where(row > col, -gates[i][0] * on_fresh[i][GROUP:], 0.0) for i in each]
    stacked = [
        jnp.concatenate([mix_terms[i].astype(bf16), key_terms[i].astype(bf16)], 0) for i in each
    ]
    direct = [mm(stacked[i], norms[i][5]) for i in each]
    turned = [
        mm_tn(stacked[i], jnp.concatenate([norms[i][4], norms[i][5]], 0)) for i in each
    ]
    for local in each:
        _, entry, last = gates[local]
        query_raw, key_raw, query_root, key_root, query, keys = norms[local]
        query_entry = entry * on_state[local][:GROUP]
        key_entry = -entry * on_state[local][GROUP:]
        key_last = last * on_adjoint[local]
        query_grad = query_entry + direct[local][:GROUP]
        key_grad = key_entry + key_last + direct[local][GROUP:] + turned[local]
        query_wide, key_wide = query.astype(f32), keys.astype(f32)
        table = mix_terms[local] * both[local][GROUP:] + key_terms[local] * both[local][:GROUP]
        last_sums = jnp.sum(key_wide * key_last, axis=1, keepdims=True)
        change = (
            jnp.sum(table + query_wide * query_entry + key_wide * key_entry, axis=1, keepdims=True)
            - last_sums
        )
        extra = jnp.sum(last_sums, axis=0, keepdims=True) + entry[GROUP - 1 :, :] * jnp.sum(
            jnp.sum(adjoints[local] * states[local], axis=0, keepdims=True), axis=1, keepdims=True
        )
        change = change + jnp.where(iota((GROUP, 1), 0) == GROUP - 1, extra, 0.0)
        change_cols = jnp.where(lane == local, change, change_cols)
        beta_cols = jnp.where(lane == local, last_sums, beta_cols)
        column_sums = jnp.where(
            sublane == local, jnp.sum(table, axis=0, keepdims=True), column_sums
        )
        query_grad = query_grad * DK ** (-0.5)
        query_dot = jnp.sum(query_grad * query_raw, axis=1, keepdims=True)
        key_dot = jnp.sum(key_grad * key_raw, axis=1, keepdims=True)
        query_back = query_root * query_grad - query_raw * (
            query_root * query_root * query_root * query_dot
        )
        key_back = key_root * key_grad - key_raw * (key_root * key_root * key_root * key_dot)
        for half in range(2):
            rows = slice(64 * half, 64 * half + 64)
            at = 2 * local + half
            y_ref[at, 0:64, :] = outputs[local][rows].astype(bf16)
            y_ref[at, 64:128, :] = query_back[rows].astype(bf16)
            y_ref[at, 128:192, :] = key_back[rows].astype(bf16)
            y_ref[at, 192:256, :] = pushed[local][rows].astype(bf16)

    after = jnp.where(row >= col, 1.0, 0.0)
    eye = jnp.where(row == col, 1.0, 0.0)
    decay_rows = exact(change_cols, after, 0, 0) - exact(column_sums, after, 1, 0)
    beta_rows = exact(beta_cols, eye, 0, 0) + column_sums
    for local in range(GRADIENT_BLOCKS):
        block = here * GRADIENT_BLOCKS + local
        decay_grad = decay_rows[local : local + 1] * gate_ref[2, pl.ds(block, 1), :]
        beta_grad = beta_rows[local : local + 1] * (1.0 - gate_ref[1, pl.ds(block, 1), :])
        rows = iota((GATE_ROWS, 128), 0)
        tail = jnp.where(rows == 0, decay_grad, jnp.where(rows == 1, beta_grad, 0.0)).astype(bf16)
        for half in range(2):
            y_ref[2 * local + half, 256:, :] = tail


def gradients(ints, received, shards, gate, column, *made):
    by_step = stepped(GRADIENT_BLOCKS, GROUP, DV)
    rows_spec = stepped(2 * GRADIENT_BLOCKS, 256 + GATE_ROWS, 128)
    return pl.pallas_call(
        gradients_kernel,
        grid=(BLOCKS // GRADIENT_BLOCKS,),
        in_specs=[
            pl.BlockSpec(memory_space=pltpu.SMEM),
            rows_spec,
            whole(SHARDS, 2 * DK, DV),
            whole(3, BLOCKS, 128),
            whole(2, 128, 128),
            *[by_step] * 4,
            stepped(GRADIENT_BLOCKS, 2, GROUP, DV),
            *[by_step] * 4,
        ],
        out_specs=rows_spec,
        out_shape=jax.ShapeDtypeStruct(received.shape, bf16),
        scratch_shapes=[pltpu.VMEM((2, DK, DV), bf16)],
        compiler_params=pltpu.CompilerParams(
            dimension_semantics=("arbitrary",), vmem_limit_bytes=LARGE_VMEM
        ),
        cost_estimate=cost(20),
        name="gradients",
    )(ints, received, shards, gate, column, *made)


def pack_kernel(query_ref, key_ref, value_ref, decay_ref, beta_ref, grad_ref, x_ref):
    decay = jnp.concatenate([decay_ref[...].astype(f32)] * 2, 1)
    beta = jnp.concatenate([beta_ref[...].astype(f32)] * 2, 1)
    rows = iota((GATE_ROWS, 128), 0)
    for head in range(PACK_HEADS):
        shared = slice(DK * (head // 2), DK * (head // 2) + DK)
        own = slice(DV * head, DV * head + DV)
        x_ref[head, 0:64, :] = query_ref[:, shared]
        x_ref[head, 64:128, :] = key_ref[:, shared]
        x_ref[head, 128:192, :] = value_ref[:, own]
        x_ref[head, 192:256, :] = grad_ref[:, own]
        x_ref[head, 256:, :] = jnp.where(
            rows == 0,
            decay[head : head + 1],
            jnp.where(rows == 1, beta[head : head + 1], 0.0),
        ).astype(bf16)


def pack(query, key, value, decay, beta, grad):
    wide = pl.BlockSpec((64, PACK_HEADS * DV), lambda i: (0, i))
    narrow = pl.BlockSpec((64, PACK_HEADS * DK // 2), lambda i: (0, i))
    gates = pl.BlockSpec((PACK_HEADS, 64), lambda i: (i, 0))
    return pl.pallas_call(
        pack_kernel,
        grid=(VALUE_HEAD_COUNT // PACK_HEADS,),
        in_specs=[narrow, narrow, wide, gates, gates, wide],
        out_specs=pl.BlockSpec((PACK_HEADS, 256 + GATE_ROWS, 128), lambda i: (i, 0, 0)),
        out_shape=jax.ShapeDtypeStruct((VALUE_HEAD_COUNT, 256 + GATE_ROWS, 128), bf16),
        compiler_params=pltpu.CompilerParams(vmem_limit_bytes=LARGE_VMEM),
        name="pack",
    )(query, key, value, decay, beta, grad)


def unpack_kernel(ints_ref, y_ref, out_ref, query_ref, key_ref, value_ref, decay_ref, beta_ref):
    for head in range(PACK_HEADS):
        own = slice(DV * head, DV * head + DV)
        out_ref[:, own] = y_ref[head, 0:64, :]
        value_ref[:, own] = y_ref[head, 192:256, :]
    for head in range(PACK_HEADS // 2):
        shared = slice(DK * head, DK * head + DK)
        for part, ref in ((1, query_ref), (2, key_ref)):
            rows = slice(64 * part, 64 * part + 64)
            summed = y_ref[2 * head, rows, :].astype(f32) + y_ref[2 * head + 1, rows, :].astype(f32)
            ref[:, shared] = summed.astype(bf16)
    tail = y_ref[:, 256:, :].astype(f32)
    rows = iota(tail.shape, 1)
    for index, ref in ((0, decay_ref), (1, beta_ref)):
        picked = jnp.sum(jnp.where(rows == index, tail, 0.0), axis=1)
        ref[...] = jnp.where(ints_ref[5] == 0, picked[:, :64], picked[:, 64:]).astype(bf16)


def unpack(ints, returned):
    wide = pl.BlockSpec((64, PACK_HEADS * DV), lambda i: (0, i))
    narrow = pl.BlockSpec((64, PACK_HEADS * DK // 2), lambda i: (0, i))
    gates = pl.BlockSpec((PACK_HEADS, 64), lambda i: (i, 0))
    wide_out = jax.ShapeDtypeStruct((64, VALUE_HEAD_COUNT * DV), bf16)
    narrow_out = jax.ShapeDtypeStruct((64, NK * DK), bf16)
    gates_out = jax.ShapeDtypeStruct((VALUE_HEAD_COUNT, 64), bf16)
    return pl.pallas_call(
        unpack_kernel,
        grid=(VALUE_HEAD_COUNT // PACK_HEADS,),
        in_specs=[
            pl.BlockSpec(memory_space=pltpu.SMEM),
            pl.BlockSpec((PACK_HEADS, 256 + GATE_ROWS, 128), lambda i: (i, 0, 0)),
        ],
        out_specs=[wide, narrow, narrow, wide, gates, gates],
        out_shape=[wide_out, narrow_out, narrow_out, wide_out, gates_out, gates_out],
        compiler_params=pltpu.CompilerParams(vmem_limit_bytes=SMALL_VMEM),
        name="unpack",
    )(ints, returned)


def local(
    query_raw,
    key_raw,
    value_raw,
    decay_raw,
    beta_raw,
    decay_base,
    decay_bias,
    doc_lengths,
    out_grad,
):
    head = lax.axis_index("head")
    shard = lax.axis_index("ctx")
    sent = pack(query_raw, key_raw, value_raw, decay_raw.T, beta_raw.T, out_grad)
    received = lax.all_to_all(sent, "head", split_axis=0, concat_axis=0, tiled=True)
    ends = [jnp.sum(doc_lengths[:j]) for j in range(4)]
    ints = jnp.stack([shard.astype(jnp.int32), *ends, (head % 2).astype(jnp.int32)])
    floats = jnp.stack(
        [
            lax.dynamic_index_in_dim(decay_base, head, keepdims=False),
            lax.dynamic_index_in_dim(decay_bias, head, keepdims=False),
        ]
    )
    send, gate, column, inverse, mixing, keys_last, fresh, *made = tables(ints, floats, received)
    shards = lax.all_to_all(send, "ctx", split_axis=0, concat_axis=0, tiled=True)
    out, push, turned = later(received, inverse, mixing, keys_last, fresh)
    back = gradients(ints, received, shards, gate, column, out, push, turned, fresh, *made)
    returned = lax.all_to_all(back, "head", split_axis=0, concat_axis=0, tiled=True)
    output, query_grad, key_grad, value_grad, decay_grad, beta_grad = unpack(ints, returned)
    return (output, query_grad, key_grad, value_grad, decay_grad.T, beta_grad.T)


def solution(mesh):
    placed = (
        P(("ctx", "head"), None),
        P(("ctx", "head"), None),
        P(("ctx", "head"), None),
        P(("ctx", "head"), None),
        P(("ctx", "head"), None),
        P(),
        P(),
        P(),
        P(("ctx", "head"), None),
    )
    return jax.shard_map(
        local,
        mesh=mesh,
        in_specs=placed,
        out_specs=(P(("ctx", "head"), None),) * 6,
        check_vma=False,
    )
```

time: 170 us -> 125 us (0.74)
  Pallas kernels: 62.3 us -> 27.6 us
  blocking collectives: 61.5 us -> 35.3 us
  waiting for transfers between devices: 23.4 us -> 38.2 us
  starting transfers between devices: 8.73 us -> 16.9 us
  local copies, waits for them, and re-layouts: 10 us -> 3.4 us
    pallas_call x4 -> x5, Pallas kernels: 62.3 us -> 27.6 us  [the longest x1 9.99 us: gradients(): pl.pallas_call(gradients_kernel, grid=(BLOCKS // GRADIENT_BLOCKS,), in_sp...]
    all_to_all x1 -> x0, blocking collectives: 24 us -> none  [local(): lax.all_to_all(send, 'ctx', split_axis=0, concat_axis=0, tiled=True)]
    all_to_all x0 -> x1, waiting for transfers between devices: none -> 13.7 us  [local(): lax.all_to_all(send, 'ctx', split_axis=0, concat_axis=0, tiled=True)]
    all_to_all x0 -> x1, starting transfers between devices: none -> 8.2 us  [local(): lax.all_to_all(send, 'ctx', split_axis=0, concat_axis=0, tiled=True)]
    unnamed x10 -> x14, local copies, waits for them, and re-layouts: 4.15 us -> 0.82 us
    pallas_call x2 -> x0, local copies, waits for them, and re-layouts: 2.78 us -> none  [unpack(): pl.pallas_call(unpack_kernel, in_specs=[pl.BlockSpec(memory_space=pltpu.S...]
    all_to_all x1, blocking collectives: 37.4 us -> 35.3 us  [local(): lax.all_to_all(back, 'head', split_axis=0, concat_axis=0, tiled=True)]
  transfers between devices with their start and end apart: 1 -> 2, of which waited for: 1 -> 2; matrix products, arithmetic and copies ran while one was open for 4% -> 4% of each run, Pallas kernels for 0% -> 3%
where the time goes in v2:
time: 125 us
  waiting for transfers between devices  38.2 us (31%)
  blocking collectives  35.3 us (28%)
  Pallas kernels  27.6 us (22%)
  starting transfers between devices  16.9 us (14%)
  local copies, waits for them, and re-layouts  3.4 us (3%)
  other arithmetic  2.63 us (2%)
    all_to_all x1, blocking collectives, local(): lax.all_to_all(back, 'head', split_axis=0, concat_axis=0, tiled=True)  35.3 us
    all_to_all x1, waiting for transfers between devices, local(): lax.all_to_all(sent, 'head', split_axis=0, concat_axis=0, tiled=True)  24.5 us
    all_to_all x1, waiting for transfers between devices, local(): lax.all_to_all(send, 'ctx', split_axis=0, concat_axis=0, tiled=True)  13.7 us
    pallas_call x1, Pallas kernels, gradients(): pl.pallas_call(gradients_kernel, grid=(BLOCKS // GRADIENT_BLOCKS,), in_sp...  9.99 us
    pallas_call x1, Pallas kernels, tables(): pl.pallas_call(tables_kernel, in_specs=[smem, smem, vmem], out_specs=[vme...  9.5 us
    all_to_all x1, starting transfers between devices, local(): lax.all_to_all(sent, 'head', split_axis=0, concat_axis=0, tiled=True)  8.73 us
    all_to_all x1, starting transfers between devices, local(): lax.all_to_all(send, 'ctx', split_axis=0, concat_axis=0, tiled=True)  8.2 us
    pallas_call x1, Pallas kernels, later(): pl.pallas_call(later_kernel, grid=(BLOCKS // LATER_BLOCKS,), in_specs=[st...  3.48 us
  transfers between devices with their start and end apart: 2, of which 2 were waited for; matrix products, arithmetic and copies ran while one was open for 4% of the time, Pallas kernels for 3%

profile of v2, /device:TPU:1, one launch (start us, length us, event | category | flops | bytes accessed | tf_op | source)
XLA Modules:
  0.0 124.7 jit_solution(4124685194723876652)
XLA Ops:
  0.6 2.8 %pack.1 = bf16[32,272,128]{2,1,0:T(8,128)(2,1)} custom-call(bf16[64,2048]{1,0:T(8,128)(2,1)} %query_ref.1, bf16[64,2048]{1,0:T(8,128)(2,1)} %key_ref.1, bf16[64,4096]{1,0:T(8,128)(2,1)} %value_ref.1, bf16[32,64]{1,0:T(8,128)(2,1)} %bitcast.9, bf16[32,64]{1,0:T(8,128)(2,1)} %bitcast.10, bf16[64,4096]{1,0:T(8,128)(2,1)} %grad_ref.1), custom_call_target="tpu_custom_call" | custom-call | tf_op jit(solution)/shard_map/pack/pallas_call | solution.py:483
  3.4 0.0 copy-start.5
  3.4 0.0 copy-start.6
  3.4 0.0 copy-start.4
  3.4 8.7 %all-to-all-start = ((bf16[32,272,128]{2,1,0:T(8,128)(2,1)}), bf16[32,272,128]{2,1,0:T(8,128)(2,1)S(1)}, u32[]{:S(2)}, u32[]{:S(2)}) async-start(bf16[32,272,128]{2,1,0:T(8,128)(2,1)} %pack.1), calls=%async_computation | async-start | bytes 4456448 | tf_op jit(solution)/shard_map/all_to_all | solution.py:547
  12.2 0.0 copy-done.5
  12.2 0.6 dynamic_slice.8
  12.8 0.0 copy-done.6
  12.8 0.6 dynamic_slice.7
  13.3 0.0 copy-done.4
  13.3 0.6 slice_reduce_fusion
  14.0 0.6 slice_reduce_fusion.1
  14.6 1.4 %stack.25.ints_ref = s32[6]{0:T(128)S(1)} concatenate(s32[1]{0:T(128)} %bitcast, s32[1]{0:T(128)} %constant.26.clone.1, s32[1]{0:T(128)S(1)} %bitcast.11, s32[1]{0:T(128)} %bitcast.1, s32[1]{0:T(128)} %bitcast.2, s32[1]{0:T(128)} %bitcast.3), dimensions={0} | concatenate | bytes 48 | tf_op jit(solution)/shard_map/stack | solution.py:549
  16.0 0.0 copy-start.1
  16.0 1.4 %pad_maximum_fusion.floats_ref = f32[2]{0:T(128)S(1)} fusion(f32[1]{0:T(128)} %dynamic_slice.8, f32[1]{0:T(128)} %dynamic_slice.7), kind=kLoop, calls=%fused_computation | loop fusion | flops 2 | bytes 16 | tf_op jit(solution)/shard_map/stack | solution.py:550
  17.4 24.5 %all-to-all-done.x_ref = bf16[32,272,128]{2,1,0:T(8,128)(2,1)S(1)} async-done(((bf16[32,272,128]{2,1,0:T(8,128)(2,1)}), bf16[32,272,128]{2,1,0:T(8,128)(2,1)S(1)}, u32[]{:S(2)}, u32[]{:S(2)}) %all-to-all-start) | async-done | bytes 2228256 | tf_op jit(solution)/shard_map/all_to_all | solution.py:547
  41.9 0.0 copy-start
  41.9 9.5 %tables.1 = (bf16[8,256,128]{2,1,0:T(8,128)(2,1)}, f32[3,16,128]{2,1,0:T(8,128)}, f32[2,128,128]{2,1,0:T(8,128)}, bf16[16,128,128]{2,1,0:T(8,128)(2,1)}, bf16[16...) custom-call(s32[6]{0:T(128)S(1)} %stack.25.ints_ref, ...), custom_call_target="tpu_custom_call" | custom-call | flops 16106127360 | bytes 1048576 | tf_op jit(solution)/shard_map/tables/pallas_call | solution.py:258
  51.4 0.0 copy-done.1
  51.4 0.0 copy-done
  51.4 8.2 %all-to-all-start.1 = ((bf16[8,256,128]{2,1,0:T(8,128)(2,1)}), bf16[8,256,128]{2,1,0:T(8,128)(2,1)S(1)}, u32[]{:S(2)}, u32[]{:S(2)}) async-start(bf16[8,256,128]{2,1,0:T(8,128)(2,1)} %get-tuple-element.27), calls=%async_computation.1 | async-start | bytes 1048576 | tf_op jit(solution)/shard_map/all_to_all | solution.py:557
  59.6 3.5 %later.1 = (bf16[16,128,128]{2,1,0:T(8,128)(2,1)}, bf16[16,128,128]{2,1,0:T(8,128)(2,1)}, bf16[16,128,128]{2,1,0:T(8,128)(2,1)}) custom-call(bf16[32,272,128]{2,1,0:T(8,128)(2,1)} %copy-done, bf16[16,128,128]{2,1,0:T(8,128)(2,1)} %get-tuple-element.30.inverse_ref, bf16[16,128,128]{2,1,0:T(8,128)(2,1)} %get-tuple-element.31.mixing_ref, ...), custom_call_target="tpu_custom_call" | custom-call | flops 2147483648 | bytes 1048576 | tf_op jit(solution)/shard_map/later/pallas_call | solution.py:293
  63.1 13.7 %all-to-all-done.1.shards_ref = bf16[8,256,128]{2,1,0:T(8,128)(2,1)S(1)} async-done(((bf16[8,256,128]{2,1,0:T(8,128)(2,1)}), bf16[8,256,128]{2,1,0:T(8,128)(2,1)S(1)}, u32[]{:S(2)}, u32[]{:S(2)}) %all-to-all-start.1) | async-done | bytes 524320 | tf_op jit(solution)/shard_map/all_to_all | solution.py:557
  76.8 0.0 copy-start.3
  76.8 0.8 copy-done.3
  77.6 10.0 %gradients.1 = bf16[32,272,128]{2,1,0:T(8,128)(2,1)} custom-call(s32[6]{0:T(128)} %copy-done.1, bf16[32,272,128]{2,1,0:T(8,128)(2,1)} %copy-done, bf16[8,256,128]{2,1,0:T(8,128)(2,1)} %copy-done.3, f32[3,16,128]{2,1,0:T(8,128)} %get-tuple-element.28.gate_ref, f32[2,128,128]{2,1,0:T(8,128)} %get-tuple-element.29.column_ref, ...), custom_call_target="tpu_custom_call" | custom-call | flops 10737418240 | bytes 1048576 | tf_op jit(solution)/shard_map/gradients/pallas_call | solution.py:437
  87.6 0.0 copy-start.2
  87.6 35.3 %all_to_all.15.y_ref = bf16[32,272,128]{2,1,0:T(8,128)(2,1)S(1)} all-to-all(bf16[32,272,128]{2,1,0:T(8,128)(2,1)} %gradients.1), channel_id=1, replica_groups=mesh['ctx'=8,'head'=32] {'head'}, dimensions={0} | all-to-all | bytes 4456448 | tf_op jit(solution)/shard_map/all_to_all | solution.py:560
  122.8 0.0 copy-done.2
  122.8 1.8 %unpack.1 = (bf16[64,4096]{1,0:T(8,128)(2,1)}, bf16[64,2048]{1,0:T(8,128)(2,1)}, bf16[64,2048]{1,0:T(8,128)(2,1)}, bf16[64,4096]{1,0:T(8,128)(2,1)}, bf16[32,64]{1,0:T(8,128)(2,1)}, /*index=5*/bf16[32,64]{1,0:T(8,128)(2,1)}) custom-call(s32[6]{0:T(128)S(1)} %copy-done.2, bf16[32,272,128]{2,1,0:T(8,128)(2,1)S(1)} %all_to_all.15.y_ref), custom_call_target="tpu_custom_call" | custom-call | tf_op jit(solution)/shard_map/unpack/pallas_call | solution.py:519
Async XLA Ops:
  3.4 8.8 %copy-start.5 = (f32[32]{0:T(128)S(1)}, f32[32]{0:T(128)}, u32[]{:S(2)}) copy-start(f32[32]{0:T(128)} %param.15) | copy-start | bytes 388
  3.4 9.4 %copy-start.6 = (f32[32]{0:T(128)S(1)}, f32[32]{0:T(128)}, u32[]{:S(2)}) copy-start(f32[32]{0:T(128)} %param.14) | copy-start | bytes 388
  3.4 9.9 %copy-start.4 = (s32[4]{0:T(128)S(1)}, s32[4]{0:T(128)}, u32[]{:S(2)}) copy-start(s32[4]{0:T(128)} %param.16) | copy-start | bytes 52
  3.4 38.4 %all-to-all-start = ((bf16[32,272,128]{2,1,0:T(8,128)(2,1)}), bf16[32,272,128]{2,1,0:T(8,128)(2,1)S(1)}, u32[]{:S(2)}, u32[]{:S(2)}) async-start(bf16[32,272,128]{2,1,0:T(8,128)(2,1)} %pack.1), calls=%async_computation | async-start | bytes 4456448 | tf_op jit(solution)/shard_map/all_to_all | solution.py:547
  16.0 35.4 %copy-start.1 = (s32[6]{0:T(128)}, s32[6]{0:T(128)S(1)}, u32[]{:S(2)}) copy-start(s32[6]{0:T(128)S(1)} %stack.25.ints_ref) | copy-start | bytes 76
  41.9 9.5 %copy-start = (bf16[32,272,128]{2,1,0:T(8,128)(2,1)}, bf16[32,272,128]{2,1,0:T(8,128)(2,1)S(1)}, u32[]{:S(2)}) copy-start(bf16[32,272,128]{2,1,0:T(8,128)(2,1)S(1)} %all-to-all-done.x_ref) | copy-start | bytes 6684676
  51.4 25.4 %all-to-all-start.1 = ((bf16[8,256,128]{2,1,0:T(8,128)(2,1)}), bf16[8,256,128]{2,1,0:T(8,128)(2,1)S(1)}, u32[]{:S(2)}, u32[]{:S(2)}) async-start(bf16[8,256,128]{2,1,0:T(8,128)(2,1)} %get-tuple-element.27), calls=%async_computation.1 | async-start | bytes 1048576 | tf_op jit(solution)/shard_map/all_to_all | solution.py:557
  76.8 0.8 copy-start.3
  87.6 35.3 %copy-start.2 = (s32[6]{0:T(128)S(1)}, s32[6]{0:T(128)}, u32[]{:S(2)}) copy-start(s32[6]{0:T(128)} %copy-done.1) | copy-start | bytes 76

commit v3 on v2

--- a/solution.py
+++ b/solution.py
@@ -12,11 +12,12 @@
 DK = 128
 DV = 128
 GROUP = 128
-GATE_ROWS = 16
+GATE_ROWS = 8
 PACK_HEADS = 16
 BLOCKS = 16
 SHARDS = 8
-GRADIENT_BLOCKS = 4
+HELD = 12
+GRADIENT_BLOCKS = 8
 LATER_BLOCKS = 8
 SMALL_VMEM = 24 * 1024 * 1024
 LARGE_VMEM = 58 * 1024 * 1024
@@ -72,27 +73,20 @@
     return jnp.sum(jnp.where(lane == block, table, 0.0), axis=1, keepdims=True)
 
 
-def block_gates(block, ints_ref, gate_ref, column_ref):
+def token_tables(cumulative, beta, ints_ref):
     starts = [ints_ref[1 + j] for j in range(4)]
-    first = ints_ref[0] * 16 * GROUP + block * GROUP
-    cum_row = gate_ref[0, pl.ds(block, 1), :]
-    beta_row = gate_ref[1, pl.ds(block, 1), :]
-    cum_col = pick_column(column_ref[0], block)
-    beta_col = pick_column(column_ref[1], block)
-    seg_row = segment_of(first + iota((1, GROUP), 1), starts)
-    seg_col = segment_of(first + iota((GROUP, 1), 0), starts)
-    before = segment_of(jnp.full((1, 1), first - 1, jnp.int32), starts)
-    row, col = iota((GROUP, GROUP), 0), iota((GROUP, GROUP), 1)
-    joined = (row >= col) & (seg_col == seg_row)
-    spread = jnp.where(joined, cum_col - cum_row, 0.0)
-    weighted = jnp.where(joined, jnp.exp(spread), 0.0) * beta_row
-    entry = jnp.where(seg_col == before, jnp.exp(cum_col), 0.0)
-    cum_last = cum_col[GROUP - 1 :, :]
-    same_last = seg_col == seg_col[GROUP - 1 :, :]
-    last = (
-        jnp.where(same_last, jnp.exp(jnp.where(same_last, cum_last - cum_col, 0.0)), 0.0) * beta_col
-    )
-    return weighted, entry, last
+    row, block = iota((GROUP, 128), 0), iota((GROUP, 128), 1)
+    first = ints_ref[0] * BLOCKS * GROUP + block * GROUP
+    positions = first + row
+    segment = segment_of(positions, starts)
+    entry = jnp.where(segment == segment_of(first - 1, starts), jnp.exp(cumulative), 0.0)
+    same = segment == segment_of(first + GROUP - 1, starts)
+    spread = jnp.where(same, cumulative[GROUP - 1 :, :] - cumulative, 0.0)
+    last = jnp.where(same, jnp.exp(spread), 0.0) * beta
+    opened = jnp.zeros((GROUP, 128), jnp.int32)
+    for start in starts:
+        opened = jnp.where(positions >= start, start, opened)
+    return entry, last, (opened - first).astype(f32)
 
 
 def inverse_root(raw):
@@ -156,23 +150,26 @@
     return [one.astype(f32) + mm(one, other) for one, other in zip(held, rest)]
 
 
-def tables_kernel(
-    ints_ref,
-    floats_ref,
-    x_ref,
-    send_ref,
-    gate_ref,
-    column_ref,
-    inverse_ref,
-    mixing_ref,
-    keys_last_ref,
-    fresh_ref,
-    maps_ref,
-    prefix_ref,
-    prefix_free_ref,
-    suffix_ref,
-    suffix_free_ref,
-):
+def tables_kernel(ints_ref, floats_ref, x_ref, send_ref, gate_ref, column_ref, *rest):
+    outs, held, sems = rest[:HELD], rest[HELD : 2 * HELD], rest[2 * HELD]
+    (
+        weighted_ref,
+        strict_ref,
+        mixing_ref,
+        inverse_ref,
+        keys_last_ref,
+        fresh_ref,
+        seen_ref,
+        read_ref,
+        prefix_ref,
+        prefix_free_ref,
+        suffix_ref,
+        suffix_free_ref,
+    ) = held
+    copies = [
+        pltpu.make_async_copy(from_ref, to_ref, sems.at[k])
+        for k, (from_ref, to_ref) in enumerate(zip(held, outs))
+    ]
     tail = x_ref[:, 256:, :].astype(f32)
     paired = tail.reshape(BLOCKS, 2, GATE_ROWS, 128)
     lane = iota((BLOCKS, GATE_ROWS, 128), 2)
@@ -190,23 +187,38 @@
     gate_ref[1] = beta
     gate_ref[2] = rate * jax.nn.sigmoid(decay_raw)
     padding = jnp.zeros((128 - BLOCKS, 128), f32)
-    column_ref[0] = exact(eye, jnp.concatenate([cumulative, padding], 0), 1, 1)
-    column_ref[1] = exact(eye, jnp.concatenate([beta, padding], 0), 1, 1)
+    cum_cols = exact(eye, jnp.concatenate([cumulative, padding], 0), 1, 1)
+    beta_cols = exact(eye, jnp.concatenate([beta, padding], 0), 1, 1)
+    entry_cols, last_cols, opened_cols = token_tables(cum_cols, beta_cols, ints_ref)
+    column_ref[0] = entry_cols
+    column_ref[1] = last_cols
 
     each = range(BLOCKS)
     units = [normed(x_ref, i)[4:] for i in each]
     both = [mm_nt(jnp.concatenate([keys, query], 0), keys) for query, keys in units]
-    gates = [block_gates(i, ints_ref, gate_ref, column_ref) for i in each]
+    wide_col = col.astype(f32)
+    gates = []
+    for i in each:
+        joined = (row >= col) & (wide_col >= opened_cols[:, i : i + 1])
+        spread = jnp.where(joined, cum_cols[:, i : i + 1] - cumulative[i : i + 1], 0.0)
+        weighted = jnp.where(joined, jnp.exp(spread), 0.0) * beta[i : i + 1]
+        gates.append((weighted, entry_cols[:, i : i + 1], last_cols[:, i : i + 1]))
+        weighted_ref[i] = weighted.astype(bf16)
     stricts = [jnp.where(row > col, gate[0] * one[:GROUP], 0.0) for gate, one in zip(gates, both)]
     mixing = [(gate[0] * one[GROUP:]).astype(bf16) for gate, one in zip(gates, both)]
     for i in each:
         mixing_ref[i] = mixing[i]
+        strict_ref[i] = stricts[i].astype(bf16)
+    for k in range(0, 3):
+        copies[k].start()
     inverses = [one.astype(bf16) for one in triangular_inverses(stricts, row, col)]
     keys_entry = [(units[i][1].astype(f32) * gates[i][1]).astype(bf16) for i in each]
     keys_last = [(units[i][1].astype(f32) * gates[i][2]).astype(bf16) for i in each]
     for i in each:
         inverse_ref[i] = inverses[i]
         keys_last_ref[i] = keys_last[i]
+    for k in range(3, 5):
+        copies[k].start()
     pairs = [
         mm(inverses[i], jnp.concatenate([block_rows(x_ref, i, 2), keys_entry[i]], 1)).astype(bf16)
         for i in each
@@ -221,34 +233,62 @@
     scales = [gates[i][1][GROUP - 1 :, :] for i in each]
     for i in each:
         fresh_ref[i] = pairs[i][:, :DV]
-        maps_ref[i, 0] = seen[i]
-        maps_ref[i, 1] = reads[i]
+        seen_ref[i] = seen[i]
+        read_ref[i] = reads[i]
+    for k in range(5, 8):
+        copies[k].start()
     nothing = jnp.zeros((DK, DK), f32)
-    forward = jnp.concatenate([jnp.zeros((DK, DV), f32), eye], 1)
-    backward = forward
+    initial = jnp.concatenate([jnp.zeros((DK, DV), f32), eye], 1)
+
+    def advance(i, state):
+        return (
+            scales[i] * state
+            - mm(steps[i], state)
+            + jnp.concatenate([written[i][:, :DV], nothing], 1)
+        )
+
+    def retreat(i, state):
+        return (
+            scales[i] * state
+            - mm_tn(steps[i], state)
+            + jnp.concatenate([terms[i], nothing], 1)
+        )
+
+    middle = BLOCKS // 2
+    lows, highs = [initial], [initial]
+    low_ends, high_ends = [initial], [initial]
+    for i in range(middle):
+        lows.append(advance(i, lows[-1]))
+        highs.append(advance(middle + i, highs[-1]))
+        high_ends.append(retreat(BLOCKS - 1 - i, high_ends[-1]))
+        low_ends.append(retreat(middle - 1 - i, low_ends[-1]))
+
+    def joined_states(later_states, entry_state):
+        moved = [mm(one[:, DV:], entry_state) for one in later_states]
+        return [
+            one + jnp.concatenate([later_one[:, :DV], nothing], 1)
+            for one, later_one in zip(moved, later_states)
+        ]
+
+    forwards = lows[:middle] + joined_states(highs, lows[middle])
+    backwards = high_ends[:middle] + joined_states(low_ends, high_ends[middle])
     for i in each:
         other = BLOCKS - 1 - i
-        forward_low, backward_low = forward.astype(bf16), backward.astype(bf16)
-        prefix_free_ref[i] = forward_low[:, :DV]
-        prefix_ref[i] = forward_low[:, DV:]
-        suffix_free_ref[other] = backward_low[:, :DV]
-        suffix_ref[other] = backward_low[:, DV:]
-        forward = (
-            scales[i] * forward
-            - mm(steps[i], forward_low)
-            + jnp.concatenate([written[i][:, :DV], nothing], 1)
-        )
-        backward = (
-            scales[other] * backward
-            - mm_tn(steps[other], backward_low)
-            + jnp.concatenate([terms[other], nothing], 1)
-        )
+        prefix_free_ref[i] = forwards[i][:, :DV].astype(bf16)
+        prefix_ref[i] = forwards[i][:, DV:].astype(bf16)
+        suffix_free_ref[other] = backwards[i][:, :DV].astype(bf16)
+        suffix_ref[other] = backwards[i][:, DV:].astype(bf16)
+    forward, backward = forwards[BLOCKS], backwards[BLOCKS]
+    for k in range(8, HELD):
+        copies[k].start()
     total = forward[:, DV:].astype(bf16)
     for other in range(SHARDS):
         send_ref[other, :DK] = total
         send_ref[other, DK:] = jnp.where(
             ints_ref[0] < other, forward[:, :DV], backward[:, :DV]
         ).astype(bf16)
+    for copy in copies:
+        copy.wait()
 
 
 def tables(ints, floats, received):
@@ -258,15 +298,15 @@
     return pl.pallas_call(
         tables_kernel,
         in_specs=[smem, smem, vmem],
-        out_specs=[vmem] * 12,
+        out_specs=[vmem] * 3 + [pl.BlockSpec(memory_space=pl.ANY)] * HELD,
         out_shape=[
             jax.ShapeDtypeStruct((SHARDS, 2 * DK, DV), bf16),
             pltpu.HBM((3, BLOCKS, 128), f32),
             pltpu.HBM((2, 128, 128), f32),
-            *[half] * 4,
-            pltpu.HBM((BLOCKS, 2, GROUP, DV), bf16),
-            *[half] * 4,
+            *[half] * HELD,
         ],
+        scratch_shapes=[pltpu.VMEM((BLOCKS, DK, DV), bf16)] * HELD
+        + [pltpu.SemaphoreType.DMA((HELD,))],
         compiler_params=pltpu.CompilerParams(vmem_limit_bytes=SMALL_VMEM),
         cost_estimate=cost(30),
         name="tables",
@@ -316,8 +356,12 @@
     out_ref,
     push_ref,
     back_ref,
+    weighted_ref,
+    strict_ref,
+    mixing_ref,
     fresh_ref,
-    maps_ref,
+    seen_ref,
+    read_ref,
     prefix_ref,
     prefix_free_ref,
     suffix_ref,
@@ -354,23 +398,22 @@
     adjoints = [suffix_free_ref[i].astype(f32) + mm(suffix_ref[i], ends_ref[1]) for i in each]
     states_low = [one.astype(bf16) for one in states]
     adjoints_low = [one.astype(bf16) for one in adjoints]
-    reads = [mm(maps_ref[i].reshape(2 * GROUP, DK), states_low[i]) for i in each]
-    fresh = [(fresh_ref[i].astype(f32) - reads[i][:GROUP]).astype(bf16) for i in each]
-    outputs = [out_ref[i].astype(f32) + reads[i][GROUP:] for i in each]
+    fresh = [
+        (fresh_ref[i].astype(f32) - mm(seen_ref[i], states_low[i])).astype(bf16) for i in each
+    ]
+    outputs = [out_ref[i].astype(f32) + mm(read_ref[i], states_low[i]) for i in each]
     pushed = [push_ref[i].astype(f32) + mm(back_ref[i], adjoints_low[i]) for i in each]
     norms = [normed(x_ref, i) for i in each]
-    both = [mm_nt(jnp.concatenate([one[5], one[4]], 0), one[5]) for one in norms]
     sides = [
         jnp.concatenate([block_rows(x_ref, i, 3), pushed[i].astype(bf16)], 0) for i in each
     ]
     on_fresh = [mm_nt(sides[i], fresh[i]) for i in each]
     on_state = [mm_nt(sides[i], states_low[i]) for i in each]
     on_adjoint = [mm_nt(fresh[i], adjoints_low[i]) for i in each]
-    gates = [
-        block_gates(here * GRADIENT_BLOCKS + i, ints_ref, gate_ref, column_ref) for i in each
-    ]
-    mix_terms = [gates[i][0] * on_fresh[i][:GROUP] for i in each]
-    key_terms = [jnp.where(row > col, -gates[i][0] * on_fresh[i][GROUP:], 0.0) for i in each]
+    mix_terms = [weighted_ref[i].astype(f32) * on_fresh[i][:GROUP] for i in each]
+    key_terms = [
+        jnp.where(row > col, -weighted_ref[i].astype(f32) * on_fresh[i][GROUP:], 0.0) for i in each
+    ]
     stacked = [
         jnp.concatenate([mix_terms[i].astype(bf16), key_terms[i].astype(bf16)], 0) for i in each
     ]
@@ -379,7 +422,8 @@
         mm_tn(stacked[i], jnp.concatenate([norms[i][4], norms[i][5]], 0)) for i in each
     ]
     for local in each:
-        _, entry, last = gates[local]
+        block = here * GRADIENT_BLOCKS + local
+        entry, last = pick_column(column_ref[0], block), pick_column(column_ref[1], block)
         query_raw, key_raw, query_root, key_root, query, keys = norms[local]
         query_entry = entry * on_state[local][:GROUP]
         key_entry = -entry * on_state[local][GROUP:]
@@ -387,7 +431,10 @@
         query_grad = query_entry + direct[local][:GROUP]
         key_grad = key_entry + key_last + direct[local][GROUP:] + turned[local]
         query_wide, key_wide = query.astype(f32), keys.astype(f32)
-        table = mix_terms[local] * both[local][GROUP:] + key_terms[local] * both[local][:GROUP]
+        table = (
+            on_fresh[local][:GROUP] * mixing_ref[local].astype(f32)
+            - on_fresh[local][GROUP:] * strict_ref[local].astype(f32)
+        )
         last_sums = jnp.sum(key_wide * key_last, axis=1, keepdims=True)
         change = (
             jnp.sum(table + query_wide * query_entry + key_wide * key_entry, axis=1, keepdims=True)
@@ -443,9 +490,7 @@
             whole(SHARDS, 2 * DK, DV),
             whole(3, BLOCKS, 128),
             whole(2, 128, 128),
-            *[by_step] * 4,
-            stepped(GRADIENT_BLOCKS, 2, GROUP, DV),
-            *[by_step] * 4,
+            *[by_step] * 13,
         ],
         out_specs=rows_spec,
         out_shape=jax.ShapeDtypeStruct(received.shape, bf16),
@@ -553,10 +598,14 @@
             lax.dynamic_index_in_dim(decay_bias, head, keepdims=False),
         ]
     )
-    send, gate, column, inverse, mixing, keys_last, fresh, *made = tables(ints, floats, received)
+    send, gate, column, weighted, strict, mixing, inverse, keys_last, fresh, *made = tables(
+        ints, floats, received
+    )
     shards = lax.all_to_all(send, "ctx", split_axis=0, concat_axis=0, tiled=True)
     out, push, turned = later(received, inverse, mixing, keys_last, fresh)
-    back = gradients(ints, received, shards, gate, column, out, push, turned, fresh, *made)
+    back = gradients(
+        ints, received, shards, gate, column, out, push, turned, weighted, strict, mixing, fresh, *made
+    )
     returned = lax.all_to_all(back, "head", split_axis=0, concat_axis=0, tiled=True)
     output, query_grad, key_grad, value_grad, decay_grad, beta_grad = unpack(ints, returned)
     return (output, query_grad, key_grad, value_grad, decay_grad.T, beta_grad.T)

time: 125 us -> 122 us (0.976)
  Pallas kernels: 27.6 us -> 26 us
where the time goes in v3:
time: 122 us
  waiting for transfers between devices  37.7 us (31%)
  blocking collectives  34.5 us (28%)
  Pallas kernels  26 us (21%)
  starting transfers between devices  16.9 us (14%)
  local copies, waits for them, and re-layouts  3.4 us (3%)
  other arithmetic  2.63 us (2%)
    all_to_all x1, blocking collectives, local(): lax.all_to_all(back, 'head', split_axis=0, concat_axis=0, tiled=True)  34.5 us
    all_to_all x1, waiting for transfers between devices, local(): lax.all_to_all(sent, 'head', split_axis=0, concat_axis=0, tiled=True)  23.8 us
    all_to_all x1, waiting for transfers between devices, local(): lax.all_to_all(send, 'ctx', split_axis=0, concat_axis=0, tiled=True)  13.9 us
    pallas_call x1, Pallas kernels, gradients(): pl.pallas_call(gradients_kernel, grid=(BLOCKS // GRADIENT_BLOCKS,), in_sp...  9.08 us
    pallas_call x1, Pallas kernels, tables(): pl.pallas_call(tables_kernel, in_specs=[smem, smem, vmem], out_specs=[vme...  8.86 us
    all_to_all x1, starting transfers between devices, local(): lax.all_to_all(sent, 'head', split_axis=0, concat_axis=0, tiled=True)  8.73 us
    all_to_all x1, starting transfers between devices, local(): lax.all_to_all(send, 'ctx', split_axis=0, concat_axis=0, tiled=True)  8.19 us
    pallas_call x1, Pallas kernels, later(): pl.pallas_call(later_kernel, grid=(BLOCKS // LATER_BLOCKS,), in_specs=[st...  3.46 us
  transfers between devices with their start and end apart: 2, of which 2 were waited for; matrix products, arithmetic and copies ran while one was open for 4% of the time, Pallas kernels for 3%

profile of v3, /device:TPU:1, one launch (start us, length us, event | category | flops | bytes accessed | tf_op | source)
XLA Modules:
  0.0 121.9 jit_solution(17492454937321819714)
XLA Ops:
  0.6 2.7 %pack.1 = bf16[32,264,128]{2,1,0:T(8,128)(2,1)} custom-call(bf16[64,2048]{1,0:T(8,128)(2,1)} %query_ref.1, bf16[64,2048]{1,0:T(8,128)(2,1)} %key_ref.1, bf16[64,4096]{1,0:T(8,128)(2,1)} %value_ref.1, bf16[32,64]{1,0:T(8,128)(2,1)} %bitcast.9, bf16[32,64]{1,0:T(8,128)(2,1)} %bitcast.10, bf16[64,4096]{1,0:T(8,128)(2,1)} %grad_ref.1), custom_call_target="tpu_custom_call" | custom-call | tf_op jit(solution)/shard_map/pack/pallas_call | solution.py:528
  3.4 0.0 copy-start.5
  3.4 0.0 copy-start.6
  3.4 0.0 copy-start.4
  3.4 8.7 %all-to-all-start = ((bf16[32,264,128]{2,1,0:T(8,128)(2,1)}), bf16[32,264,128]{2,1,0:T(8,128)(2,1)S(1)}, u32[]{:S(2)}, u32[]{:S(2)}) async-start(bf16[32,264,128]{2,1,0:T(8,128)(2,1)} %pack.1), calls=%async_computation | async-start | bytes 4325376 | tf_op jit(solution)/shard_map/all_to_all | solution.py:592
  12.1 0.0 copy-done.5
  12.2 0.6 dynamic_slice.8
  12.7 0.0 copy-done.6
  12.7 0.6 dynamic_slice.7
  13.3 0.0 copy-done.4
  13.3 0.6 slice_reduce_fusion
  14.0 0.6 slice_reduce_fusion.1
  14.6 1.4 %stack.25.ints_ref = s32[6]{0:T(128)S(1)} concatenate(s32[1]{0:T(128)} %bitcast, s32[1]{0:T(128)} %constant.26.clone.1, s32[1]{0:T(128)S(1)} %bitcast.11, s32[1]{0:T(128)} %bitcast.1, s32[1]{0:T(128)} %bitcast.2, s32[1]{0:T(128)} %bitcast.3), dimensions={0} | concatenate | bytes 48 | tf_op jit(solution)/shard_map/stack | solution.py:594
  16.0 0.0 copy-start.1
  16.0 1.4 %pad_maximum_fusion.floats_ref = f32[2]{0:T(128)S(1)} fusion(f32[1]{0:T(128)} %dynamic_slice.8, f32[1]{0:T(128)} %dynamic_slice.7), kind=kLoop, calls=%fused_computation | loop fusion | flops 2 | bytes 16 | tf_op jit(solution)/shard_map/stack | solution.py:595
  17.4 23.8 %all-to-all-done.x_ref = bf16[32,264,128]{2,1,0:T(8,128)(2,1)S(1)} async-done(((bf16[32,264,128]{2,1,0:T(8,128)(2,1)}), bf16[32,264,128]{2,1,0:T(8,128)(2,1)S(1)}, u32[]{:S(2)}, u32[]{:S(2)}) %all-to-all-start) | async-done | bytes 2162720 | tf_op jit(solution)/shard_map/all_to_all | solution.py:592
  41.1 0.0 copy-start
  41.1 8.9 %tables.1 = (bf16[8,256,128]{2,1,0:T(8,128)(2,1)}, f32[3,16,128]{2,1,0:T(8,128)}, f32[2,128,128]{2,1,0:T(8,128)}, bf16[16,128,128]{2,1,0:T(8,128)(2,1)}, bf16[16...) custom-call(s32[6]{0:T(128)S(1)} %stack.25.ints_ref, ...), custom_call_target="tpu_custom_call" | custom-call | flops 16106127360 | bytes 1048576 | tf_op jit(solution)/shard_map/tables/pallas_call | solution.py:298
  50.0 0.0 copy-done.1
  50.0 0.0 copy-done
  50.0 8.2 %all-to-all-start.1 = ((bf16[8,256,128]{2,1,0:T(8,128)(2,1)}), bf16[8,256,128]{2,1,0:T(8,128)(2,1)S(1)}, u32[]{:S(2)}, u32[]{:S(2)}) async-start(bf16[8,256,128]{2,1,0:T(8,128)(2,1)} %get-tuple-element.30), calls=%async_computation.1 | async-start | bytes 1048576 | tf_op jit(solution)/shard_map/all_to_all | solution.py:604
  58.2 3.5 %later.1 = (bf16[16,128,128]{2,1,0:T(8,128)(2,1)}, bf16[16,128,128]{2,1,0:T(8,128)(2,1)}, bf16[16,128,128]{2,1,0:T(8,128)(2,1)}) custom-call(bf16[32,264,128]{2,1,0:T(8,128)(2,1)} %copy-done, bf16[16,128,128]{2,1,0:T(8,128)(2,1)} %get-tuple-element.33.inverse_ref, bf16[16,128,128]{2,1,0:T(8,128)(2,1)} %get-tuple-element.34.mixing_ref, ...), custom_call_target="tpu_custom_call" | custom-call | flops 2147483648 | bytes 1048576 | tf_op jit(solution)/shard_map/later/pallas_call | solution.py:333
  61.7 13.9 %all-to-all-done.1.shards_ref = bf16[8,256,128]{2,1,0:T(8,128)(2,1)S(1)} async-done(((bf16[8,256,128]{2,1,0:T(8,128)(2,1)}), bf16[8,256,128]{2,1,0:T(8,128)(2,1)S(1)}, u32[]{:S(2)}, u32[]{:S(2)}) %all-to-all-start.1) | async-done | bytes 524320 | tf_op jit(solution)/shard_map/all_to_all | solution.py:604
  75.6 0.0 copy-start.3
  75.6 0.8 copy-done.3
  76.4 9.1 %gradients.1 = bf16[32,264,128]{2,1,0:T(8,128)(2,1)} custom-call(s32[6]{0:T(128)} %copy-done.1, bf16[32,264,128]{2,1,0:T(8,128)(2,1)} %copy-done, bf16[8,256,128]{2,1,0:T(8,128)(2,1)} %copy-done.3, f32[3,16,128]{2,1,0:T(8,128)} %get-tuple-element.31.gate_ref, f32[2,128,128]{2,1,0:T(8,128)} %get-tuple-element.32.column_ref, ...), custom_call_target="tpu_custom_call" | custom-call | flops 10737418240 | bytes 1048576 | tf_op jit(solution)/shard_map/gradients/pallas_call | solution.py:484
  85.5 0.0 copy-start.2
  85.5 34.5 %all_to_all.15.y_ref = bf16[32,264,128]{2,1,0:T(8,128)(2,1)S(1)} all-to-all(bf16[32,264,128]{2,1,0:T(8,128)(2,1)} %gradients.1), channel_id=1, replica_groups=mesh['ctx'=8,'head'=32] {'head'}, dimensions={0} | all-to-all | bytes 4325376 | tf_op jit(solution)/shard_map/all_to_all | solution.py:609
  120.0 0.0 copy-done.2
  120.0 1.8 %unpack.1 = (bf16[64,4096]{1,0:T(8,128)(2,1)}, bf16[64,2048]{1,0:T(8,128)(2,1)}, bf16[64,2048]{1,0:T(8,128)(2,1)}, bf16[64,4096]{1,0:T(8,128)(2,1)}, bf16[32,64]{1,0:T(8,128)(2,1)}, /*index=5*/bf16[32,64]{1,0:T(8,128)(2,1)}) custom-call(s32[6]{0:T(128)S(1)} %copy-done.2, bf16[32,264,128]{2,1,0:T(8,128)(2,1)S(1)} %all_to_all.15.y_ref), custom_call_target="tpu_custom_call" | custom-call | tf_op jit(solution)/shard_map/unpack/pallas_call | solution.py:564
Async XLA Ops:
  3.4 8.8 %copy-start.5 = (f32[32]{0:T(128)S(1)}, f32[32]{0:T(128)}, u32[]{:S(2)}) copy-start(f32[32]{0:T(128)} %param.15) | copy-start | bytes 388
  3.4 9.4 %copy-start.6 = (f32[32]{0:T(128)S(1)}, f32[32]{0:T(128)}, u32[]{:S(2)}) copy-start(f32[32]{0:T(128)} %param.14) | copy-start | bytes 388
  3.4 9.9 %copy-start.4 = (s32[4]{0:T(128)S(1)}, s32[4]{0:T(128)}, u32[]{:S(2)}) copy-start(s32[4]{0:T(128)} %param.16) | copy-start | bytes 52
  3.4 37.7 %all-to-all-start = ((bf16[32,264,128]{2,1,0:T(8,128)(2,1)}), bf16[32,264,128]{2,1,0:T(8,128)(2,1)S(1)}, u32[]{:S(2)}, u32[]{:S(2)}) async-start(bf16[32,264,128]{2,1,0:T(8,128)(2,1)} %pack.1), calls=%async_computation | async-start | bytes 4325376 | tf_op jit(solution)/shard_map/all_to_all | solution.py:592
  16.0 34.0 %copy-start.1 = (s32[6]{0:T(128)}, s32[6]{0:T(128)S(1)}, u32[]{:S(2)}) copy-start(s32[6]{0:T(128)S(1)} %stack.25.ints_ref) | copy-start | bytes 76
  41.1 8.9 %copy-start = (bf16[32,264,128]{2,1,0:T(8,128)(2,1)}, bf16[32,264,128]{2,1,0:T(8,128)(2,1)S(1)}, u32[]{:S(2)}) copy-start(bf16[32,264,128]{2,1,0:T(8,128)(2,1)S(1)} %all-to-all-done.x_ref) | copy-start | bytes 6488068
  50.0 25.6 %all-to-all-start.1 = ((bf16[8,256,128]{2,1,0:T(8,128)(2,1)}), bf16[8,256,128]{2,1,0:T(8,128)(2,1)S(1)}, u32[]{:S(2)}, u32[]{:S(2)}) async-start(bf16[8,256,128]{2,1,0:T(8,128)(2,1)} %get-tuple-element.30), calls=%async_computation.1 | async-start | bytes 1048576 | tf_op jit(solution)/shard_map/all_to_all | solution.py:604
  75.6 0.8 copy-start.3
  85.5 34.5 %copy-start.2 = (s32[6]{0:T(128)S(1)}, s32[6]{0:T(128)}, u32[]{:S(2)}) copy-start(s32[6]{0:T(128)} %copy-done.1) | copy-start | bytes 76

commit v4 on v3

--- a/solution.py
+++ b/solution.py
@@ -12,7 +12,7 @@
 DK = 128
 DV = 128
 GROUP = 128
-GATE_ROWS = 8
+GATE_ROWS = 16
 PACK_HEADS = 16
 BLOCKS = 16
 SHARDS = 8
@@ -21,6 +21,7 @@
 LATER_BLOCKS = 8
 SMALL_VMEM = 24 * 1024 * 1024
 LARGE_VMEM = 58 * 1024 * 1024
+GRADIENT_VMEM = 53 * 1024 * 1024
 
 bf16 = jnp.bfloat16
 f32 = jnp.float32
@@ -374,16 +375,35 @@
     @pl.when(here == 0)
     def prologue():
         me = ints_ref[0]
-        state = jnp.zeros((DK, DV), f32)
-        adjoint = jnp.zeros((DK, DV), f32)
-        for k in range(7):
-            moved = mm(shards_ref[k, :DK], split_two(state))
-            new = moved[:, :DV] + moved[:, DV:] + shards_ref[k, DK:].astype(f32)
-            state = jnp.where(k < me, new, state)
-            at = 7 - k
-            moved = mm_tn(shards_ref[at, :DK], split_two(adjoint))
-            new = moved[:, :DV] + moved[:, DV:] + shards_ref[at, DK:].astype(f32)
-            adjoint = jnp.where(at > me, new, adjoint)
+        eye = eye_of(DK)
+        nothing = jnp.zeros((DK, DV), f32)
+
+        def step(at, used, turned, pair):
+            low = pair.astype(bf16)
+            rest = (pair - low.astype(f32)).astype(bf16)
+            product = mm_tn if turned else mm
+            moved = product(shards_ref[at, :DK], low) + product(shards_ref[at, :DK], rest)
+            added = shards_ref[at, DK:].astype(f32)
+            width = pair.shape[1]
+            if width > DV:
+                added = jnp.concatenate([added, jnp.zeros((DK, width - DV), f32)], 1)
+            return jnp.where(used, moved + added, pair)
+
+        early, late = nothing, jnp.concatenate([nothing, eye], 1)
+        early_end, late_end = nothing, late
+        for k in range(4):
+            early = step(k, k < me, False, early)
+            early_end = step(7 - k, 7 - k > me, True, early_end)
+            if k < 3:
+                late = step(4 + k, 4 + k < me, False, late)
+                late_end = step(3 - k, 3 - k > me, True, late_end)
+
+        def joined(late, early):
+            moved = mm(late[:, DV:], split_two(early))
+            return late[:, :DV] + moved[:, :DV] + moved[:, DV:]
+
+        state = joined(late, early)
+        adjoint = joined(late_end, early_end)
         ends_ref[0] = state.astype(bf16)
         ends_ref[1] = adjoint.astype(bf16)
 
@@ -496,7 +516,7 @@
         out_shape=jax.ShapeDtypeStruct(received.shape, bf16),
         scratch_shapes=[pltpu.VMEM((2, DK, DV), bf16)],
         compiler_params=pltpu.CompilerParams(
-            dimension_semantics=("arbitrary",), vmem_limit_bytes=LARGE_VMEM
+            dimension_semantics=("arbitrary",), vmem_limit_bytes=GRADIENT_VMEM
         ),
         cost_estimate=cost(20),
         name="gradients",

time: 122 us -> 122 us (level)
  no operation moved by 1% of the time
where the time goes in v4:
time: 122 us
  waiting for transfers between devices  38.1 us (31%)
  blocking collectives  35.3 us (29%)
  Pallas kernels  25.5 us (21%)
  starting transfers between devices  16.9 us (14%)
  other arithmetic  2.63 us (2%)
  local copies, waits for them, and re-layouts  2.61 us (2%)
    all_to_all x1, blocking collectives, local(): lax.all_to_all(back, 'head', split_axis=0, concat_axis=0, tiled=True)  35.3 us
    all_to_all x1, waiting for transfers between devices, local(): lax.all_to_all(sent, 'head', split_axis=0, concat_axis=0, tiled=True)  24.5 us
    all_to_all x1, waiting for transfers between devices, local(): lax.all_to_all(send, 'ctx', split_axis=0, concat_axis=0, tiled=True)  13.6 us
    pallas_call x1, Pallas kernels, tables(): pl.pallas_call(tables_kernel, in_specs=[smem, smem, vmem], out_specs=[vme...  8.88 us
    all_to_all x1, starting transfers between devices, local(): lax.all_to_all(sent, 'head', split_axis=0, concat_axis=0, tiled=True)  8.73 us
    pallas_call x1, Pallas kernels, gradients(): pl.pallas_call(gradients_kernel, grid=(BLOCKS // GRADIENT_BLOCKS,), in_sp...  8.54 us
    all_to_all x1, starting transfers between devices, local(): lax.all_to_all(send, 'ctx', split_axis=0, concat_axis=0, tiled=True)  8.2 us
    pallas_call x1, Pallas kernels, later(): pl.pallas_call(later_kernel, grid=(BLOCKS // LATER_BLOCKS,), in_specs=[st...  3.52 us
  transfers between devices with their start and end apart: 2, of which 2 were waited for; matrix products, arithmetic and copies ran while one was open for 4% of the time, Pallas kernels for 3%

profile of v4, /device:TPU:1, one launch (start us, length us, event | category | flops | bytes accessed | tf_op | source)
XLA Modules:
  0.0 121.8 jit_solution(10946849728865682880)
XLA Ops:
  0.6 2.8 %pack.1 = bf16[32,272,128]{2,1,0:T(8,128)(2,1)} custom-call(bf16[64,2048]{1,0:T(8,128)(2,1)} %query_ref.1, bf16[64,2048]{1,0:T(8,128)(2,1)} %key_ref.1, bf16[64,4096]{1,0:T(8,128)(2,1)} %value_ref.1, bf16[32,64]{1,0:T(8,128)(2,1)} %bitcast.9, bf16[32,64]{1,0:T(8,128)(2,1)} %bitcast.10, bf16[64,4096]{1,0:T(8,128)(2,1)} %grad_ref.1), custom_call_target="tpu_custom_call" | custom-call | tf_op jit(solution)/shard_map/pack/pallas_call | solution.py:548
  3.4 0.0 copy-start.4
  3.4 0.0 copy-start.5
  3.4 0.0 copy-start.3
  3.4 8.7 %all-to-all-start = ((bf16[32,272,128]{2,1,0:T(8,128)(2,1)}), bf16[32,272,128]{2,1,0:T(8,128)(2,1)S(1)}, u32[]{:S(2)}, u32[]{:S(2)}) async-start(bf16[32,272,128]{2,1,0:T(8,128)(2,1)} %pack.1), calls=%async_computation | async-start | bytes 4456448 | tf_op jit(solution)/shard_map/all_to_all | solution.py:612
  12.2 0.0 copy-done.4
  12.2 0.6 dynamic_slice.8
  12.8 0.0 copy-done.5
  12.8 0.6 dynamic_slice.7
  13.3 0.0 copy-done.3
  13.4 0.6 slice_reduce_fusion
  14.0 0.6 slice_reduce_fusion.1
  14.6 1.4 %stack.25.ints_ref = s32[6]{0:T(128)S(1)} concatenate(s32[1]{0:T(128)} %bitcast, s32[1]{0:T(128)} %constant.26.clone.1, s32[1]{0:T(128)S(1)} %bitcast.11, s32[1]{0:T(128)} %bitcast.1, s32[1]{0:T(128)} %bitcast.2, s32[1]{0:T(128)} %bitcast.3), dimensions={0} | concatenate | bytes 48 | tf_op jit(solution)/shard_map/stack | solution.py:614
  16.0 1.4 %pad_maximum_fusion.floats_ref = f32[2]{0:T(128)S(1)} fusion(f32[1]{0:T(128)} %dynamic_slice.8, f32[1]{0:T(128)} %dynamic_slice.7), kind=kLoop, calls=%fused_computation | loop fusion | flops 2 | bytes 16 | tf_op jit(solution)/shard_map/stack | solution.py:615
  17.4 24.5 %all-to-all-done.x_ref = bf16[32,272,128]{2,1,0:T(8,128)(2,1)S(1)} async-done(((bf16[32,272,128]{2,1,0:T(8,128)(2,1)}), bf16[32,272,128]{2,1,0:T(8,128)(2,1)S(1)}, u32[]{:S(2)}, u32[]{:S(2)}) %all-to-all-start) | async-done | bytes 2228256 | tf_op jit(solution)/shard_map/all_to_all | solution.py:612
  41.9 0.0 copy-start
  41.9 8.9 %tables.1 = (bf16[8,256,128]{2,1,0:T(8,128)(2,1)}, f32[3,16,128]{2,1,0:T(8,128)}, f32[2,128,128]{2,1,0:T(8,128)}, bf16[16,128,128]{2,1,0:T(8,128)(2,1)}, bf16[16...) custom-call(s32[6]{0:T(128)S(1)} %stack.25.ints_ref, ...), custom_call_target="tpu_custom_call" | custom-call | flops 16106127360 | bytes 1048576 | tf_op jit(solution)/shard_map/tables/pallas_call | solution.py:299
  50.8 0.0 copy-done
  50.8 8.2 %all-to-all-start.1 = ((bf16[8,256,128]{2,1,0:T(8,128)(2,1)}), bf16[8,256,128]{2,1,0:T(8,128)(2,1)S(1)}, u32[]{:S(2)}, u32[]{:S(2)}) async-start(bf16[8,256,128]{2,1,0:T(8,128)(2,1)} %get-tuple-element.30), calls=%async_computation.1 | async-start | bytes 1048576 | tf_op jit(solution)/shard_map/all_to_all | solution.py:624
  59.0 0.0 copy-start.1
  59.0 0.0 copy-start.2
  59.0 3.5 %later.1 = (bf16[16,128,128]{2,1,0:T(8,128)(2,1)}, bf16[16,128,128]{2,1,0:T(8,128)(2,1)}, bf16[16,128,128]{2,1,0:T(8,128)(2,1)}) custom-call(bf16[32,272,128]{2,1,0:T(8,128)(2,1)} %copy-done, bf16[16,128,128]{2,1,0:T(8,128)(2,1)} %get-tuple-element.33.inverse_ref, bf16[16,128,128]{2,1,0:T(8,128)(2,1)} %get-tuple-element.34.mixing_ref, ...), custom_call_target="tpu_custom_call" | custom-call | flops 2147483648 | bytes 1048576 | tf_op jit(solution)/shard_map/later/pallas_call | solution.py:334
  62.5 13.6 %all-to-all-done.1.shards_ref = bf16[8,256,128]{2,1,0:T(8,128)(2,1)S(1)} async-done(((bf16[8,256,128]{2,1,0:T(8,128)(2,1)}), bf16[8,256,128]{2,1,0:T(8,128)(2,1)S(1)}, u32[]{:S(2)}, u32[]{:S(2)}) %all-to-all-start.1) | async-done | bytes 524320 | tf_op jit(solution)/shard_map/all_to_all | solution.py:624
  76.1 0.0 copy-done.1
  76.1 0.0 copy-done.2
  76.1 8.5 %gradients.1 = bf16[32,272,128]{2,1,0:T(8,128)(2,1)} custom-call(s32[6]{0:T(128)S(1)} %stack.25.ints_ref, bf16[32,272,128]{2,1,0:T(8,128)(2,1)} %copy-done, bf16[8,256,128]{2,1,0:T(8,128)(2,1)S(1)} %all-to-all-done.1.shards_ref, f32[3,16,128]{2,1,0:T(8,128)S(1)} %copy-done.2, f32[2,128,128]{2,1,0:T(8,128)S(1)} %copy-done.1, ...), custom_call_target="tpu_custom_call" | custom-call | flops 10737418240 | bytes 1048576 | tf_op jit(solution)/shard_map/gradients/pallas_call | solution.py:504
  84.6 35.3 %all_to_all.15.y_ref = bf16[32,272,128]{2,1,0:T(8,128)(2,1)S(1)} all-to-all(bf16[32,272,128]{2,1,0:T(8,128)(2,1)} %gradients.1), channel_id=1, replica_groups=mesh['ctx'=8,'head'=32] {'head'}, dimensions={0} | all-to-all | bytes 4456448 | tf_op jit(solution)/shard_map/all_to_all | solution.py:629
  120.0 1.8 %unpack.1 = (bf16[64,4096]{1,0:T(8,128)(2,1)}, bf16[64,2048]{1,0:T(8,128)(2,1)}, bf16[64,2048]{1,0:T(8,128)(2,1)}, bf16[64,4096]{1,0:T(8,128)(2,1)}, bf16[32,64]{1,0:T(8,128)(2,1)}, /*index=5*/bf16[32,64]{1,0:T(8,128)(2,1)}) custom-call(s32[6]{0:T(128)S(1)} %stack.25.ints_ref, bf16[32,272,128]{2,1,0:T(8,128)(2,1)S(1)} %all_to_all.15.y_ref), custom_call_target="tpu_custom_call" | custom-call | tf_op jit(solution)/shard_map/unpack/pallas_call | solution.py:584
Async XLA Ops:
  3.4 8.8 %copy-start.4 = (f32[32]{0:T(128)S(1)}, f32[32]{0:T(128)}, u32[]{:S(2)}) copy-start(f32[32]{0:T(128)} %param.15) | copy-start | bytes 388
  3.4 9.4 %copy-start.5 = (f32[32]{0:T(128)S(1)}, f32[32]{0:T(128)}, u32[]{:S(2)}) copy-start(f32[32]{0:T(128)} %param.14) | copy-start | bytes 388
  3.4 9.9 %copy-start.3 = (s32[4]{0:T(128)S(1)}, s32[4]{0:T(128)}, u32[]{:S(2)}) copy-start(s32[4]{0:T(128)} %param.16) | copy-start | bytes 52
  3.4 38.4 %all-to-all-start = ((bf16[32,272,128]{2,1,0:T(8,128)(2,1)}), bf16[32,272,128]{2,1,0:T(8,128)(2,1)S(1)}, u32[]{:S(2)}, u32[]{:S(2)}) async-start(bf16[32,272,128]{2,1,0:T(8,128)(2,1)} %pack.1), calls=%async_computation | async-start | bytes 4456448 | tf_op jit(solution)/shard_map/all_to_all | solution.py:612
  41.9 8.9 %copy-start = (bf16[32,272,128]{2,1,0:T(8,128)(2,1)}, bf16[32,272,128]{2,1,0:T(8,128)(2,1)S(1)}, u32[]{:S(2)}) copy-start(bf16[32,272,128]{2,1,0:T(8,128)(2,1)S(1)} %all-to-all-done.x_ref) | copy-start | bytes 6684676
  50.8 25.3 %all-to-all-start.1 = ((bf16[8,256,128]{2,1,0:T(8,128)(2,1)}), bf16[8,256,128]{2,1,0:T(8,128)(2,1)S(1)}, u32[]{:S(2)}, u32[]{:S(2)}) async-start(bf16[8,256,128]{2,1,0:T(8,128)(2,1)} %get-tuple-element.30), calls=%async_computation.1 | async-start | bytes 1048576 | tf_op jit(solution)/shard_map/all_to_all | solution.py:624
  59.0 17.1 %copy-start.1 = (f32[2,128,128]{2,1,0:T(8,128)S(1)}, f32[2,128,128]{2,1,0:T(8,128)}, u32[]{:S(2)}) copy-start(f32[2,128,128]{2,1,0:T(8,128)} %get-tuple-element.32.column_ref) | copy-start | bytes 393220
  59.0 17.1 %copy-start.2 = (f32[3,16,128]{2,1,0:T(8,128)S(1)}, f32[3,16,128]{2,1,0:T(8,128)}, u32[]{:S(2)}) copy-start(f32[3,16,128]{2,1,0:T(8,128)} %get-tuple-element.31.gate_ref) | copy-start | bytes 73732
